TPU v7x, 32 devices: a whole 2x2x4 slice. The times are simulated.
32 devices in a mesh: row: 4 (over z), col: 8 (over y, x, core).
Axes of the slice: x: 2, y: 2, z: 4, core: 2. Of those that a mesh axis runs over, the one named last changes fastest.
Arguments:
- multipliers: bfloat16 [128, 32768], P('col', 'row'), may hold values from -6 to 6
- source: float32 [128, 32768], P('col', 'row'), may hold values from -6 to 6
- denominator: float32 [128, 32768], P('col', 'row'), may hold values from 0.8 to 6
- cycle: bfloat16 [32768, 32768], P('col', 'row'), may hold values from -0.03125 to 0.03125
Outputs:
- updated: bfloat16 [128, 32768], P('col', 'row')
All inputs are finite; a program needn't handle non-finite values.
Results may differ from a plain program's by a relative error of at most 0.015.
Values may be sent and summed in bfloat16 or wider, within the bound.
No kernel may reach another device: no remote copies, remote signals or barrier semaphores. Data moves between devices by JAX's collectives and lax.ppermute only.
A program may use at most 128 MiB of HBM per device.

v0:
```python
import jax
import jax.numpy as jnp
from jax import lax
from jax.sharding import PartitionSpec as P

ITERS = 2


def realign(current):
    gathered = lax.all_gather(current, "row", axis=1, tiled=True)
    return lax.all_to_all(gathered, "col", split_axis=1, concat_axis=0, tiled=True)


def shards(multipliers, source, denominator, cycle):
    current = multipliers
    local_rows = multipliers.shape[0]
    for sweep in range(ITERS):
        aligned = realign(current)

        def project_rows(row_start, row_count, aligned=aligned):
            return jnp.dot(aligned, cycle, preferred_element_type=jnp.float32)

        product = lax.psum_scatter(
            project_rows(jnp.int32(0), local_rows * lax.axis_size("col")).astype(jnp.bfloat16),
            "col",
            scatter_dimension=0,
            tiled=True,
        ).astype(jnp.float32)
        current = ((source + product) / denominator).astype(jnp.bfloat16)
    return current


def solution(mesh):
    placed = (P("col", "row"), P("col", "row"), P("col", "row"), P("col", "row"))
    return jax.shard_map(
        shards, mesh=mesh, in_specs=placed, out_specs=P("col", "row"), check_vma=False
    )
```

profile of v0, /device:TPU:0, one launch (start us, length us, event | category | flops | bytes accessed | tf_op | source)
XLA Modules:
  0.0 244.7 jit_solution(5490826275806045272)
XLA Ops:
  6.5 0.0 copy-start
  6.5 0.0 copy-start.1
  6.5 0.0 all-gather.3.cloned.1.call-start
  6.5 0.7 all-gather.3.cloned.1.call-update
  7.3 0.0 reduce-scatter.3.cloned.1.call-start
  7.3 32.3 %all-gather.3.cloned.1.call-done = bf16[16,32768]{1,0:T(8,128)(2,1)} async-done(((bf16[16,8192]{1,0:T(8,128)(2,1)}), bf16[16,32768]{1,0:T(8,128)(2,1)}) %all-gather.3.cloned.1.call-update) | async-done | bytes 1048592 | tf_op jit(solution)/shard_map/all_gather | solution.py:10
  39.6 1.3 copy.15
  40.9 18.8 %all_to_all.38 = bf16[16,8,4096]{2,0,1:T(8,128)(2,1)S(1)} all-to-all(bf16[16,8,4096]{2,0,1:T(8,128)(2,1)S(1)} %bitcast.20), channel_id=1, replica_groups=mesh['row'=4,'col'=8] {'col'}, dimensions={1} | all-to-all | bytes 2097152 | tf_op jit(solution)/shard_map/all_to_all | solution.py:11
  59.7 24.3 %convolution_convert_fusion.1 = bf16[128,8192]{1,0:T(8,128)(2,1)} fusion(bf16[128,4096]{1,0:T(8,128)(2,1)S(1)} %bitcast.18, bf16[4096,8192]{1,0:T(8,128)(2,1)} %param.7), kind=kOutput, calls=%fused_computation.1 | convolution fusion | flops 8590983168 | bytes 70254592 | tf_op jit(solution)/shard_map/dot_general | solution.py:21
  84.0 0.0 reduce-scatter.3.cloned.1.call-update
  84.0 0.0 all-gather.5.cloned.1.call-start
  84.1 39.0 %reduce-scatter.3.cloned.1.call-done = bf16[16,8192]{1,0:T(8,128)(2,1)} async-done(((bf16[128,8192]{1,0:T(8,128)(2,1)}), bf16[16,8192]{1,0:T(8,128)(2,1)}) %reduce-scatter.3.cloned.1.call-update) | async-done | bytes 262160 | tf_op jit(solution)/shard_map/reduce_scatter | solution.py:23
  123.1 0.0 copy-done
  123.1 0.0 copy-done.1
  123.1 1.7 divide_convert_fusion.1
  124.8 0.0 all-gather.5.cloned.1.call-update
  124.9 0.0 reduce-scatter.5.cloned.1.call-start
  124.9 28.0 %all-gather.5.cloned.1.call-done = bf16[16,32768]{1,0:T(8,128)(2,1)} async-done(((bf16[16,8192]{1,0:T(8,128)(2,1)}), bf16[16,32768]{1,0:T(8,128)(2,1)}) %all-gather.5.cloned.1.call-update) | async-done | bytes 1048592 | tf_op jit(solution)/shard_map/all_gather | solution.py:10
  152.9 1.3 copy.14
  154.2 18.8 %all_to_all.39 = bf16[16,8,4096]{2,0,1:T(8,128)(2,1)S(1)} all-to-all(bf16[16,8,4096]{2,0,1:T(8,128)(2,1)S(1)} %bitcast.21), channel_id=1, replica_groups=mesh['row'=4,'col'=8] {'col'}, dimensions={1} | all-to-all | bytes 2097152 | tf_op jit(solution)/shard_map/all_to_all | solution.py:11
  173.1 24.3 %convolution_convert_fusion = bf16[128,8192]{1,0:T(8,128)(2,1)} fusion(bf16[128,4096]{1,0:T(8,128)(2,1)S(1)} %bitcast.19, bf16[4096,8192]{1,0:T(8,128)(2,1)} %param.7), kind=kOutput, calls=%fused_computation | convolution fusion | flops 8590983168 | bytes 70254592 | tf_op jit(solution)/shard_map/dot_general | solution.py:21
  197.4 0.0 reduce-scatter.5.cloned.1.call-update
  197.4 39.1 %reduce-scatter.5.cloned.1.call-done = bf16[16,8192]{1,0:T(8,128)(2,1)} async-done(((bf16[128,8192]{1,0:T(8,128)(2,1)}), bf16[16,8192]{1,0:T(8,128)(2,1)}) %reduce-scatter.5.cloned.1.call-update) | async-done | bytes 262160 | tf_op jit(solution)/shard_map/reduce_scatter | solution.py:23
  236.5 1.7 divide_convert_fusion
Async XLA Ops:
  6.5 116.6 %copy-start = (f32[16,8192]{1,0:T(8,128)S(1)}, f32[16,8192]{1,0:T(8,128)}, u32[]{:S(2)}) copy-start(f32[16,8192]{1,0:T(8,128)} %param.6) | copy-start | bytes 1572868
  6.5 116.6 %copy-start.1 = (f32[16,8192]{1,0:T(8,128)S(1)}, f32[16,8192]{1,0:T(8,128)}, u32[]{:S(2)}) copy-start(f32[16,8192]{1,0:T(8,128)} %param.5) | copy-start | bytes 1572868
  6.5 33.1 %all-gather.3.cloned.1.call-start = ((), (), s32[]{:S(2)}) async-start(), calls=%async_computation.4 | async-start | bytes 1310720 | tf_op jit(solution)/shard_map/all_gather | solution.py:10
  7.3 115.8 %reduce-scatter.3.cloned.1.call-start = ((), (), s32[]{:S(2)}) async-start(), calls=%async_computation.5 | async-start | bytes 2359296 | tf_op jit(solution)/shard_map/reduce_scatter | solution.py:23
  84.0 68.9 %all-gather.5.cloned.1.call-start = ((), (), s32[]{:S(2)}) async-start(), calls=%async_computation.6 | async-start | bytes 1310720 | tf_op jit(solution)/shard_map/all_gather | solution.py:10
  124.9 111.6 %reduce-scatter.5.cloned.1.call-start = ((), (), s32[]{:S(2)}) async-start(), calls=%async_computation.7 | async-start | bytes 2359296 | tf_op jit(solution)/shard_map/reduce_scatter | solution.py:23
Sparse Core Ops, SparseCore 0:
  8.9 30.6 all-gather.2
  84.2 38.8 reduce-scatter.2
  125.0 27.9 all-gather.4
  197.5 38.9 reduce-scatter.4
where the time goes:
time: 245 us
  waiting for transfers between devices  139 us (57%)
  matrix products  48.6 us (20%)
  blocking collectives  37.6 us (15%)
  between operations  13.1 us (5%)
  other arithmetic  3.47 us (1%)
  local copies, waits for them, and re-layouts  2.59 us (1%)
    reduce_scatter x2, waiting for transfers between devices, shards(): lax.psum_scatter(project_rows(jnp.int32(0), local_rows * lax.axis_size('c...  78.1 us
    all_gather x2, waiting for transfers between devices, realign(): gathered = lax.all_gather(current, 'row', axis=1, tiled=True)  60.3 us
    dot_general x2, matrix products, project_rows(): return jnp.dot(aligned, cycle, preferred_element_type=jnp.float32)  48.6 us
    all_to_all x2, blocking collectives, realign(): lax.all_to_all(gathered, 'col', split_axis=1, concat_axis=0, tiled=True)  37.6 us
  transfers between devices with their start and end apart: 4, of which 4 were waited for; matrix products, arithmetic and copies ran while one was open for 0% of the time, Pallas kernels for 0%

commit v1 on v0

v1 whole, which is shorter than its diff:
```python
import jax
import jax.numpy as jnp
from jax import lax
from jax.experimental import pallas as pl
from jax.experimental.pallas import tpu as pltpu
from jax.sharding import PartitionSpec as P

ITERS = 2
CORES = 2
HELD_BYTES = 32 << 20
LIMIT_BYTES = 8 << 20
TILE = 512
PIECE_ROWS = 512

VMEM = pl.BlockSpec(memory_space=pltpu.VMEM)
HBM = pl.BlockSpec(memory_space=pl.ANY)


def hold(cycle, start):
    rows, cols = cycle.shape[0] - start, cycle.shape[1]
    count = rows // PIECE_ROWS

    def kernel(cycle_ref, *refs):
        copies = [
            pltpu.make_async_copy(
                cycle_ref.at[pl.ds(start + index * PIECE_ROWS, PIECE_ROWS)], refs[index], refs[count].at[index]
            )
            for index in range(count)
        ]
        for copy in copies:
            copy.start()
        for copy in copies:
            copy.wait()

    return pl.pallas_call(
        kernel,
        in_specs=[HBM],
        out_specs=[VMEM] * count,
        out_shape=[pltpu.VMEM((PIECE_ROWS, cols), cycle.dtype)] * count,
        scratch_shapes=[pltpu.SemaphoreType.DMA((count,))],
        compiler_params=pltpu.CompilerParams(vmem_limit_bytes=1 << 20),
        cost_estimate=pl.CostEstimate(flops=0, bytes_accessed=2 * rows * cols * 2, transcendentals=0),
        name="hold",
    )(cycle)


def project(blocks, held, cycle, base_of, width, finish, outs, name):
    count = len(blocks)
    block_rows, depth = blocks[0].shape
    pieces = len(held)
    streamed = depth - pieces * PIECE_ROWS
    tile = min(TILE, width)
    steps = width // tile

    def kernel(*refs):
        block_refs = refs[:count]
        held_refs, cycle_ref = refs[count : count + pieces], refs[count + pieces]
        out_refs = refs[count + pieces + 1 : count + pieces + 1 + len(outs)]
        lhs, buffer, sems = refs[count + pieces + 1 + len(outs) :]
        base = base_of()

        def columns(step):
            return pl.ds(pl.multiple_of(base + step * tile, tile), tile)

        def fetch(step):
            return pltpu.make_async_copy(
                cycle_ref.at[pl.ds(0, streamed), columns(step)], buffer.at[lax.rem(step, 2)], sems.at[lax.rem(step, 2)]
            )

        if streamed:
            for step in range(min(2, steps)):
                fetch(jnp.int32(step)).start()
        for index in range(count):
            lhs[index * block_rows : (index + 1) * block_rows, :] = block_refs[index][...]
        def body(step, carry):
            total = 0.0
            for index, held_ref in enumerate(held_refs):
                at = streamed + index * PIECE_ROWS
                total += jnp.dot(
                    lhs[:, at : at + PIECE_ROWS], held_ref[:, columns(step)], preferred_element_type=jnp.float32
                )
            if streamed:
                fetch(step).wait()
                total += jnp.dot(lhs[:, :streamed], buffer[lax.rem(step, 2)], preferred_element_type=jnp.float32)

                @pl.when(step + 2 < steps)
                def _():
                    fetch(step + 2).start()

            finish(total, pl.ds(pl.multiple_of(step * tile, tile), tile), out_refs)
            return carry

        lax.fori_loop(0, steps, body, 0)

    rows = count * block_rows
    return pl.pallas_call(
        kernel,
        in_specs=[VMEM] * (count + pieces) + [HBM],
        out_specs=[VMEM] * len(outs),
        out_shape=outs,
        scratch_shapes=[
            pltpu.VMEM((rows, depth), jnp.bfloat16),
            pltpu.VMEM((2, max(streamed, 16), tile), jnp.bfloat16),
            pltpu.SemaphoreType.DMA((2,)),
        ],
        compiler_params=pltpu.CompilerParams(vmem_limit_bytes=LIMIT_BYTES),
        cost_estimate=pl.CostEstimate(
            flops=2 * rows * depth * width, bytes_accessed=2 * streamed * width, transcendentals=0
        ),
        name=name,
    )(*blocks, *held, cycle)


def add_split(keep, received, slot_of, count, name):
    rows, width = keep.shape
    block_rows = rows // count

    def kernel(keep_ref, received_ref, *out_refs):
        for k in range(count):
            at = pl.ds(pl.multiple_of(slot_of(k) * block_rows, block_rows), block_rows)
            total = keep_ref[at, :] + received_ref[at, :].astype(jnp.float32)
            out_refs[k][...] = total.astype(out_refs[k].dtype)

    outs = [jax.ShapeDtypeStruct((block_rows, width), jnp.float32)]
    outs += [jax.ShapeDtypeStruct((block_rows, width), jnp.bfloat16)] * (count - 1)
    return pl.pallas_call(
        kernel,
        in_specs=[VMEM] * 2,
        out_specs=[VMEM] * count,
        out_shape=outs,
        compiler_params=pltpu.CompilerParams(vmem_limit_bytes=LIMIT_BYTES),
        cost_estimate=pl.CostEstimate(flops=rows * width, bytes_accessed=8 * rows * width, transcendentals=0),
        name=name,
    )(keep, received)


def shards(multipliers, source, denominator, cycle):
    planes, lanes = lax.axis_size("row"), lax.axis_size("col")
    chips = lanes // CORES
    local_rows, local_cols = multipliers.shape
    half = local_cols // CORES
    depth = cycle.shape[0]
    block_rows = local_rows * CORES
    total_rows = local_rows * lanes

    def place():
        lane = lax.axis_index("col")
        return lax.axis_index("row"), lane // CORES, lax.rem(lane, CORES)

    plane, chip, core = place()
    first = core == 0
    core_swap = [(i, i ^ 1) for i in range(lanes)]
    chip_swap = [[(i, i ^ (k * CORES)) for i in range(lanes)] for k in range(chips)]
    turn = [
        [
            ((z * chips + p) * CORES + c, ((p ^ k) * chips + z) * CORES + c)
            for z in range(planes)
            for p in range(chips)
            for c in range(CORES)
        ]
        for k in range(planes)
    ]

    def pair(array):
        low, high = array[:, :half], array[:, half:]
        mine = jnp.where(first, low, high)
        theirs = lax.ppermute(jnp.where(first, high, low), "col", core_swap)
        return jnp.concatenate(
            [jnp.where(first, mine, theirs), jnp.where(first, theirs, mine)], axis=0
        )

    def slot_of(k):
        z, p, _ = place()
        return z ^ p ^ k

    def scatter_add(keep, received, name):
        own, *others = add_split(keep, received, slot_of, chips, name)
        parts = [own]
        for k in range(1, chips):
            parts.append(lax.ppermute(others[k - 1], "col", chip_swap[k]).astype(jnp.float32))
        return sum(parts[1:], parts[0])

    def realign(current):
        return [lax.ppermute(current, ("row", "col"), turn[k]) for k in range(planes)]

    per_row = local_cols * 2
    held_rows = min(depth, HELD_BYTES // per_row) // PIECE_ROWS * PIECE_ROWS
    held = hold(cycle, depth - held_rows)
    current = pair(multipliers)
    source_pair, denominator_pair = pair(source), pair(denominator)

    for sweep in range(ITERS):
        blocks = realign(current)
        if sweep < ITERS - 1:
            def store(total, at, out_refs):
                out_refs[0][:, at] = total.astype(out_refs[0].dtype)

            send, = project(
                blocks, held, cycle, lambda: (1 - place()[2]) * half, half, store,
                [jax.ShapeDtypeStruct((total_rows, half), jnp.bfloat16)], "project_send",
            )
            received = lax.ppermute(send, "col", core_swap)
            keep, = project(
                blocks, held, cycle, lambda: place()[2] * half, half, store,
                [jax.ShapeDtypeStruct((total_rows, half), jnp.float32)], "project_keep",
            )
            product = scatter_add(keep, received, "add_columns")
            current = ((source_pair + product) / denominator_pair).astype(jnp.bfloat16)
        else:
            def store(total, at, out_refs):
                mine = place()[2] == 0
                for index in range(chips):
                    row = index * block_rows
                    low, high = total[row : row + local_rows], total[row + local_rows : row + block_rows]
                    to = slice(index * local_rows, (index + 1) * local_rows)
                    out_refs[0][to, at] = jnp.where(mine, low, high)
                    out_refs[1][to, at] = jnp.where(mine, high, low).astype(jnp.bfloat16)

            keep, send = project(
                blocks, held, cycle, lambda: 0, local_cols, store,
                [
                    jax.ShapeDtypeStruct((total_rows // CORES, local_cols), jnp.float32),
                    jax.ShapeDtypeStruct((total_rows // CORES, local_cols), jnp.bfloat16),
                ], "project_rows",
            )
            received = lax.ppermute(send, "col", core_swap)
            product = scatter_add(keep, received, "add_rows")
            current = ((source + product) / denominator).astype(jnp.bfloat16)
    return current


def solution(mesh):
    placed = (P("col", "row"), P("col", "row"), P("col", "row"), P("col", "row"))
    return jax.shard_map(
        shards, mesh=mesh, in_specs=placed, out_specs=P("col", "row"), check_vma=False
    )
```

time: 245 us -> 143 us (0.58)
  waiting for transfers between devices: 139 us -> 39 us
  Pallas kernels: 0 us -> 48.7 us
  matrix products: 48.6 us -> 0 us
  starting transfers between devices: 0.13 us -> 45.6 us
  blocking collectives: 37.6 us -> 0 us
  between operations: 13.1 us -> 0.23 us
    reduce_scatter x2 -> x0, waiting for transfers between devices: 78.1 us -> none  [shards(): lax.psum_scatter(project_rows(jnp.int32(0), local_rows * lax.axis_size('c...]
    all_gather x2 -> x0, waiting for transfers between devices: 60.3 us -> none  [realign(): gathered = lax.all_gather(current, 'row', axis=1, tiled=True)]
    pallas_call x0 -> x6, Pallas kernels: none -> 48.7 us  [the longest x3 37.8 us: project(): pl.pallas_call(kernel, in_specs=[VMEM] * (count + pieces) + [HBM], out_sp...]
    dot_general x2 -> x0, matrix products: 48.6 us -> none  [project_rows(): return jnp.dot(aligned, cycle, preferred_element_type=jnp.float32)]
    ppermute x0 -> x19, starting transfers between devices: none -> 45.6 us  [the longest x6 24.9 us: scatter_add(): lax.ppermute(others[k - 1], 'col', chip_swap[k]).astype(jnp.float32)]
    ppermute x0 -> x19, waiting for transfers between devices: none -> 39 us  [the longest x6 24.1 us: scatter_add(): lax.ppermute(others[k - 1], 'col', chip_swap[k]).astype(jnp.float32)]
    all_to_all x2 -> x0, blocking collectives: 37.6 us -> none  [realign(): lax.all_to_all(gathered, 'col', split_axis=1, concat_axis=0, tiled=True)]
    select_n x0 -> x6, other arithmetic: none -> 4.19 us  [the longest x3 3.1 us: pair(): theirs = lax.ppermute(jnp.where(first, high, low), 'col', core_swap)]
  transfers between devices with their start and end apart: 4 -> 19, of which waited for: 4 -> 8; matrix products, arithmetic and copies ran while one was open for 0% -> 2% of each run, Pallas kernels for 0% -> 22%
where the time goes in v1:
time: 143 us; the launch traced here: 142 us
  Pallas kernels  48.7 us (34%)
  starting transfers between devices  45.6 us (32%)
  waiting for transfers between devices  39 us (27%)
  other arithmetic  5.3 us (4%)
  local copies, waits for them, and re-layouts  3.4 us (2%)
    pallas_call x3, Pallas kernels, project(): pl.pallas_call(kernel, in_specs=[VMEM] * (count + pieces) + [HBM], out_sp...  37.8 us
    ppermute x6, starting transfers between devices, scatter_add(): lax.ppermute(others[k - 1], 'col', chip_swap[k]).astype(jnp.float32)  24.9 us
    ppermute x6, waiting for transfers between devices, scatter_add(): lax.ppermute(others[k - 1], 'col', chip_swap[k]).astype(jnp.float32)  24.1 us
    ppermute x8, starting transfers between devices, realign(): lax.ppermute(current, ('row', 'col'), turn[k])  19.9 us
    ppermute x8, waiting for transfers between devices, realign(): lax.ppermute(current, ('row', 'col'), turn[k])  12.2 us
    pallas_call x1, Pallas kernels, hold(): pl.pallas_call(kernel, in_specs=[HBM], out_specs=[VMEM] * count, out_shap...  10.6 us
    unnamed x8, local copies, waits for them, and re-layouts  3.4 us
    select_n x3, other arithmetic, pair(): theirs = lax.ppermute(jnp.where(first, high, low), 'col', core_swap)  3.1 us
  transfers between devices with their start and end apart: 19, of which 8 were waited for; matrix products, arithmetic and copies ran while one was open for 2% of the time, Pallas kernels for 22%

profile of v1, /device:TPU:0, one launch (start us, length us, event | category | flops | bytes accessed | tf_op | source)
XLA Modules:
  0.0 142.3 jit_solution(15272413138652592643)
XLA Ops:
  0.0 1.0 broadcast_select_fusion.4
  1.0 0.5 collective-permute-start.1
  1.5 1.1 slice_select_fusion
  2.6 0.1 collective-permute-start.10
  2.7 0.0 collective-permute-done.1
  2.7 1.0 broadcast_select_fusion.3
  3.7 0.7 collective-permute-start.2
  4.4 5.7 %collective-permute-start.3 = (bf16[32,4096]{1,0:T(8,128)(2,1)S(1)}, bf16[32,4096]{1,0:T(8,128)(2,1)S(1)}, u32[]{:S(2)}, u32[]{:S(2)}) collective-permute-start(bf16[32,4096]{1,0:T(8,128)(2,1)S(1)} %pad_maximum_fusion), channel_id=1, source_target_pairs={{0,8},{1,9},{2,0},{3,1},{4,24},{5,25},{6,16},{7,17},{8,10},{9,11},... | collective-permute-start | bytes 786440 | tf_op jit(solution)/shard_map/ppermute | solution.py:184
  10.1 3.5 %collective-permute-start.4 = (bf16[32,4096]{1,0:T(8,128)(2,1)S(1)}, bf16[32,4096]{1,0:T(8,128)(2,1)S(1)}, u32[]{:S(2)}, u32[]{:S(2)}) collective-permute-start(bf16[32,4096]{1,0:T(8,128)(2,1)S(1)} %pad_maximum_fusion), channel_id=1, source_target_pairs={{0,16},{1,17},{2,24},{3,25},{4,0},{5,1},{6,8},{7,9},{8,18},{9,19},... | collective-permute-start | bytes 786440 | tf_op jit(solution)/shard_map/ppermute | solution.py:184
  13.6 1.9 %collective-permute-start.5 = (bf16[32,4096]{1,0:T(8,128)(2,1)S(1)}, bf16[32,4096]{1,0:T(8,128)(2,1)S(1)}, u32[]{:S(2)}, u32[]{:S(2)}) collective-permute-start(bf16[32,4096]{1,0:T(8,128)(2,1)S(1)} %pad_maximum_fusion), channel_id=1, source_target_pairs={{0,24},{1,25},{2,16},{3,17},{4,8},{5,9},{6,0},{7,1},{8,26},{9,27},... | collective-permute-start | bytes 786440 | tf_op jit(solution)/shard_map/ppermute | solution.py:184
  15.5 1.1 slice_select_fusion.2
  16.6 10.6 %hold.1 = (bf16[512,8192]{1,0:T(8,128)(2,1)S(1)}, bf16[512,8192]{1,0:T(8,128)(2,1)S(1)}, bf16[512,8192]{1,0:T(8,128)(2,1)S(1)}, bf16[512,8192]{1,0:T(8,128)(2,1)S(1)}) custom-call(bf16[4096,8192]{1,0:T(8,128)(2,1)} %refs_8_.5), custom_call_target="tpu_custom_call" | custom-call | bytes 67108864 | tf_op jit(solution)/shard_map/hold/pallas_call | solution.py:35
  27.1 0.0 copy-start
  27.2 0.0 collective-permute-done.2.refs_0_
  27.2 0.1 collective-permute-start
  27.2 0.0 collective-permute-done.3.refs_1_
  27.3 0.0 collective-permute-done.4.refs_2_
  27.3 0.0 collective-permute-done.5.refs_3_
  27.3 0.0 copy-start.2
  27.3 11.6 %project_send.1 = bf16[128,4096]{1,0:T(8,128)(2,1)S(1)} custom-call(bf16[32,4096]{1,0:T(8,128)(2,1)S(1)} %collective-permute-done.2.refs_0_, bf16[32,4096]{1,0:T(8,128)(2,1)S(1)} %collective-permute-done.3.refs_1_, bf16[32,4096]{1,0:T(8,128)(2,1)S(1)} %collective-permute-done.4.refs_2_, bf16[32,4096]{1,0:T(8,128)(2,1)S(1)} %collective-permute-done.5.refs_3_, ...), custom_call_target="tpu_custom_call" | custom-call | flops 4294967296 | bytes 16777216 | tf_op jit(solution)/shard_map/project_send/pallas_call | solution.py:96
  38.9 0.1 collective-permute-start.6
  39.0 0.0 collective-permute-done.10
  39.0 0.0 copy-done.2
  39.1 0.0 copy-done
  39.1 0.0 copy-start.3
  39.1 9.0 %project_keep.1.keep_ref = f32[128,4096]{1,0:T(8,128)S(1)} custom-call(bf16[32,4096]{1,0:T(8,128)(2,1)S(1)} %collective-permute-done.2.refs_0_, bf16[32,4096]{1,0:T(8,128)(2,1)S(1)} %collective-permute-done.3.refs_1_, bf16[32,4096]{1,0:T(8,128)(2,1)S(1)} %collective-permute-done.4.refs_2_, bf16[32,4096]{1,0:T(8,128)(2,1)S(1)} %collective-permute-done.5.refs_3_, ...), custom_call_target="tpu_custom_call" | custom-call | flops 4294967296 | bytes 16777216 | tf_op jit(solution)/shard_map/project_keep/pallas_call | solution.py:96
  48.2 0.0 collective-permute-done.6.received_ref
  48.2 0.2 add_columns.1
  48.4 1.6 %collective-permute-start.7 = (bf16[32,4096]{1,0:T(8,128)(2,1)S(1)}, bf16[32,4096]{1,0:T(8,128)(2,1)S(1)}, u32[]{:S(2)}, u32[]{:S(2)}) collective-permute-start(bf16[32,4096]{1,0:T(8,128)(2,1)S(1)} %get-tuple-element.24), channel_id=1, source_target_pairs={{0,2},{1,3},{2,0},{3,1},{4,6},{5,7},{6,4},{7,5},{8,10},{9,11},{10,... | collective-permute-start | bytes 786440 | tf_op jit(solution)/shard_map/ppermute | solution.py:180
  50.0 8.5 %collective-permute-start.8 = (bf16[32,4096]{1,0:T(8,128)(2,1)S(1)}, bf16[32,4096]{1,0:T(8,128)(2,1)S(1)}, u32[]{:S(2)}, u32[]{:S(2)}) collective-permute-start(bf16[32,4096]{1,0:T(8,128)(2,1)S(1)} %get-tuple-element.25), channel_id=1, source_target_pairs={{0,4},{1,5},{2,6},{3,7},{4,0},{5,1},{6,2},{7,3},{8,12},{9,13},{10,... | collective-permute-start | bytes 786440 | tf_op jit(solution)/shard_map/ppermute | solution.py:180
  58.5 1.4 collective-permute-start.9
  59.9 0.0 collective-permute-done
  59.9 0.0 copy-done.3
  59.9 0.0 collective-permute-done.7
  59.9 10.4 %collective-permute-done.8 = bf16[32,4096]{1,0:T(8,128)(2,1)S(1)} collective-permute-done((bf16[32,4096]{1,0:T(8,128)(2,1)S(1)}, bf16[32,4096]{1,0:T(8,128)(2,1)S(1)}, u32[]{:S(2)}, u32[]{:S(2)}) %collective-permute-start.8) | collective-permute-done | bytes 262176 | tf_op jit(solution)/shard_map/ppermute | solution.py:180
  70.3 1.8 %collective-permute-done.9 = bf16[32,4096]{1,0:T(8,128)(2,1)S(1)} collective-permute-done((bf16[32,4096]{1,0:T(8,128)(2,1)S(1)}, bf16[32,4096]{1,0:T(8,128)(2,1)S(1)}, u32[]{:S(2)}, u32[]{:S(2)}) %collective-permute-start.9) | collective-permute-done | bytes 262176 | tf_op jit(solution)/shard_map/ppermute | solution.py:180
  72.1 0.2 fusion.1
  72.3 0.7 collective-permute-start.11
  73.0 3.3 %collective-permute-start.12 = (bf16[32,4096]{1,0:T(8,128)(2,1)S(1)}, bf16[32,4096]{1,0:T(8,128)(2,1)S(1)}, u32[]{:S(2)}, u32[]{:S(2)}) collective-permute-start(bf16[32,4096]{1,0:T(8,128)(2,1)S(1)} %fusion.1), channel_id=1, source_target_pairs={{0,8},{1,9},{2,0},{3,1},{4,24},{5,25},{6,16},{7,17},{8,10},{9,11},... | collective-permute-start | bytes 786440 | tf_op jit(solution)/shard_map/ppermute | solution.py:184
  76.3 2.6 %collective-permute-start.13 = (bf16[32,4096]{1,0:T(8,128)(2,1)S(1)}, bf16[32,4096]{1,0:T(8,128)(2,1)S(1)}, u32[]{:S(2)}, u32[]{:S(2)}) collective-permute-start(bf16[32,4096]{1,0:T(8,128)(2,1)S(1)} %fusion.1), channel_id=1, source_target_pairs={{0,16},{1,17},{2,24},{3,25},{4,0},{5,1},{6,8},{7,9},{8,18},{9,19},... | collective-permute-start | bytes 786440 | tf_op jit(solution)/shard_map/ppermute | solution.py:184
  79.0 1.5 %collective-permute-start.14 = (bf16[32,4096]{1,0:T(8,128)(2,1)S(1)}, bf16[32,4096]{1,0:T(8,128)(2,1)S(1)}, u32[]{:S(2)}, u32[]{:S(2)}) collective-permute-start(bf16[32,4096]{1,0:T(8,128)(2,1)S(1)} %fusion.1), channel_id=1, source_target_pairs={{0,24},{1,25},{2,16},{3,17},{4,8},{5,9},{6,0},{7,1},{8,26},{9,27},... | collective-permute-start | bytes 786440 | tf_op jit(solution)/shard_map/ppermute | solution.py:184
  80.5 0.0 collective-permute-done.11.refs_0_
  80.5 2.6 %collective-permute-done.12.refs_1_ = bf16[32,4096]{1,0:T(8,128)(2,1)S(1)} collective-permute-done((bf16[32,4096]{1,0:T(8,128)(2,1)S(1)}, bf16[32,4096]{1,0:T(8,128)(2,1)S(1)}, u32[]{:S(2)}, u32[]{:S(2)}) %collective-permute-start.12) | collective-permute-done | bytes 262176 | tf_op jit(solution)/shard_map/ppermute | solution.py:184
  83.1 8.6 %collective-permute-done.13.refs_2_ = bf16[32,4096]{1,0:T(8,128)(2,1)S(1)} collective-permute-done((bf16[32,4096]{1,0:T(8,128)(2,1)S(1)}, bf16[32,4096]{1,0:T(8,128)(2,1)S(1)}, u32[]{:S(2)}, u32[]{:S(2)}) %collective-permute-start.13) | collective-permute-done | bytes 262176 | tf_op jit(solution)/shard_map/ppermute | solution.py:184
  91.7 1.1 collective-permute-done.14.refs_3_
  92.7 0.0 copy-start.1
  92.7 3.4 %copy-done.1 = bf16[512,8192]{1,0:T(8,128)(2,1)S(1)} copy-done((bf16[512,8192]{1,0:T(8,128)(2,1)S(1)}, bf16[512,8192]{1,0:T(8,128)(2,1)}, u32[]{:S(2)}) %copy-start.1) | copy-done | bytes 8388632
  96.1 17.1 %project_rows.1 = (f32[64,8192]{1,0:T(8,128)S(1)}, bf16[64,8192]{1,0:T(8,128)(2,1)S(1)}) custom-call(bf16[32,4096]{1,0:T(8,128)(2,1)S(1)} %collective-permute-done.11.refs_0_, bf16[32,4096]{1,0:T(8,128)(2,1)S(1)} %collective-permute-done.12.refs_1_, bf16[32,4096]{1,0:T(8,128)(2,1)S(1)} %collective-permute-done.13.refs_2_, ...), custom_call_target="tpu_custom_call" | custom-call | flops 8589934592 | bytes 33554432 | tf_op jit(solution)/shard_map/project_rows/pallas_call | solution.py:96
  113.2 0.1 collective-permute-start.15
  113.2 2.6 %collective-permute-done.15.received_ref = bf16[64,8192]{1,0:T(8,128)(2,1)S(1)} collective-permute-done((bf16[64,8192]{1,0:T(8,128)(2,1)S(1)}, bf16[64,8192]{1,0:T(8,128)(2,1)S(1)}, u32[]{:S(2)}, u32[]{:S(2)}) %collective-permute-start.15) | collective-permute-done | bytes 1048608 | tf_op jit(solution)/shard_map/ppermute | solution.py:226
  115.9 0.2 add_rows.1
  116.1 2.0 %collective-permute-start.16 = (bf16[16,8192]{1,0:T(8,128)(2,1)S(1)}, bf16[16,8192]{1,0:T(8,128)(2,1)S(1)}, u32[]{:S(2)}, u32[]{:S(2)}) collective-permute-start(bf16[16,8192]{1,0:T(8,128)(2,1)S(1)} %get-tuple-element.30), channel_id=1, source_target_pairs={{0,2},{1,3},{2,0},{3,1},{4,6},{5,7},{6,4},{7,5},{8,10},{9,11},{10,... | collective-permute-start | bytes 786440 | tf_op jit(solution)/shard_map/ppermute | solution.py:180
  118.1 10.0 %collective-permute-start.17 = (bf16[16,8192]{1,0:T(8,128)(2,1)S(1)}, bf16[16,8192]{1,0:T(8,128)(2,1)S(1)}, u32[]{:S(2)}, u32[]{:S(2)}) collective-permute-start(bf16[16,8192]{1,0:T(8,128)(2,1)S(1)} %get-tuple-element.31), channel_id=1, source_target_pairs={{0,4},{1,5},{2,6},{3,7},{4,0},{5,1},{6,2},{7,3},{8,12},{9,13},{10,... | collective-permute-start | bytes 786440 | tf_op jit(solution)/shard_map/ppermute | solution.py:180
  128.1 1.4 collective-permute-start.18
  129.5 0.0 collective-permute-done.16
  129.5 10.1 %collective-permute-done.17 = bf16[16,8192]{1,0:T(8,128)(2,1)S(1)} collective-permute-done((bf16[16,8192]{1,0:T(8,128)(2,1)S(1)}, bf16[16,8192]{1,0:T(8,128)(2,1)S(1)}, u32[]{:S(2)}, u32[]{:S(2)}) %collective-permute-start.17) | collective-permute-done | bytes 262176 | tf_op jit(solution)/shard_map/ppermute | solution.py:180
  139.6 1.8 %collective-permute-done.18 = bf16[16,8192]{1,0:T(8,128)(2,1)S(1)} collective-permute-done((bf16[16,8192]{1,0:T(8,128)(2,1)S(1)}, bf16[16,8192]{1,0:T(8,128)(2,1)S(1)}, u32[]{:S(2)}, u32[]{:S(2)}) %collective-permute-start.18) | collective-permute-done | bytes 262176 | tf_op jit(solution)/shard_map/ppermute | solution.py:180
  141.4 0.9 divide_convert_fusion
  (3 shorter events, 0.1 us)
Async XLA Ops:
  1.0 1.7 %collective-permute-start.1 = (bf16[16,4096]{1,0:T(8,128)(2,1)S(1)}, bf16[16,4096]{1,0:T(8,128)(2,1)S(1)}, u32[]{:S(2)}, u32[]{:S(2)}) collective-permute-start(bf16[16,4096]{1,0:T(8,128)(2,1)S(1)} %broadcast_select_fusion.4), channel_id=1, source_target_pairs={{0,1},{1,0},{2,3},{3,2},{4,5},{5,4},{6,7},{7,6},{8,9},{9,8},{10,11... | collective-permute-start | bytes 393224 | tf_op jit(solution)/shard_map/ppermute | solution.py:167
  2.6 36.5 %collective-permute-start.10 = (f32[16,4096]{1,0:T(8,128)S(1)}, f32[16,4096]{1,0:T(8,128)S(1)}, u32[]{:S(2)}, u32[]{:S(2)}) collective-permute-start(f32[16,4096]{1,0:T(8,128)S(1)} %slice_select_fusion), channel_id=1, source_target_pairs={{0,1},{1,0},{2,3},{3,2},{4,5},{5,4},{6,7},{7,6},{8,9},{9,8},{10,11... | collective-permute-start | bytes 786440 | tf_op jit(solution)/shard_map/ppermute | solution.py:167
  3.7 23.4 %collective-permute-start.2 = (bf16[32,4096]{1,0:T(8,128)(2,1)S(1)}, bf16[32,4096]{1,0:T(8,128)(2,1)S(1)}, u32[]{:S(2)}, u32[]{:S(2)}) collective-permute-start(bf16[32,4096]{1,0:T(8,128)(2,1)S(1)} %pad_maximum_fusion), channel_id=1, source_target_pairs={{0,0},{1,1},{2,8},{3,9},{4,16},{5,17},{6,24},{7,25},{8,2},{9,3},{1... | collective-permute-start | bytes 786440 | tf_op jit(solution)/shard_map/ppermute | solution.py:184
  4.4 22.8 %collective-permute-start.3 = (bf16[32,4096]{1,0:T(8,128)(2,1)S(1)}, bf16[32,4096]{1,0:T(8,128)(2,1)S(1)}, u32[]{:S(2)}, u32[]{:S(2)}) collective-permute-start(bf16[32,4096]{1,0:T(8,128)(2,1)S(1)} %pad_maximum_fusion), channel_id=1, source_target_pairs={{0,8},{1,9},{2,0},{3,1},{4,24},{5,25},{6,16},{7,17},{8,10},{9,11},... | collective-permute-start | bytes 786440 | tf_op jit(solution)/shard_map/ppermute | solution.py:184
  10.1 17.2 %collective-permute-start.4 = (bf16[32,4096]{1,0:T(8,128)(2,1)S(1)}, bf16[32,4096]{1,0:T(8,128)(2,1)S(1)}, u32[]{:S(2)}, u32[]{:S(2)}) collective-permute-start(bf16[32,4096]{1,0:T(8,128)(2,1)S(1)} %pad_maximum_fusion), channel_id=1, source_target_pairs={{0,16},{1,17},{2,24},{3,25},{4,0},{5,1},{6,8},{7,9},{8,18},{9,19},... | collective-permute-start | bytes 786440 | tf_op jit(solution)/shard_map/ppermute | solution.py:184
  13.6 13.7 %collective-permute-start.5 = (bf16[32,4096]{1,0:T(8,128)(2,1)S(1)}, bf16[32,4096]{1,0:T(8,128)(2,1)S(1)}, u32[]{:S(2)}, u32[]{:S(2)}) collective-permute-start(bf16[32,4096]{1,0:T(8,128)(2,1)S(1)} %pad_maximum_fusion), channel_id=1, source_target_pairs={{0,24},{1,25},{2,16},{3,17},{4,8},{5,9},{6,0},{7,1},{8,26},{9,27},... | collective-permute-start | bytes 786440 | tf_op jit(solution)/shard_map/ppermute | solution.py:184
  27.1 12.0 %copy-start = (bf16[512,8192]{1,0:T(8,128)(2,1)}, bf16[512,8192]{1,0:T(8,128)(2,1)S(1)}, u32[]{:S(2)}) copy-start(bf16[512,8192]{1,0:T(8,128)(2,1)S(1)} %get-tuple-element.21.refs_6_) | copy-start | bytes 25165828
  27.2 32.7 %collective-permute-start = (f32[16,4096]{1,0:T(8,128)S(1)}, f32[16,4096]{1,0:T(8,128)S(1)}, u32[]{:S(2)}, u32[]{:S(2)}) collective-permute-start(f32[16,4096]{1,0:T(8,128)S(1)} %slice_select_fusion.2), channel_id=1, source_target_pairs={{0,1},{1,0},{2,3},{3,2},{4,5},{5,4},{6,7},{7,6},{8,9},{9,8},{10,11... | collective-permute-start | bytes 786440 | tf_op jit(solution)/shard_map/ppermute | solution.py:167
  27.3 11.8 %copy-start.2 = (f32[16,8192]{1,0:T(8,128)S(1)}, f32[16,8192]{1,0:T(8,128)}, u32[]{:S(2)}) copy-start(f32[16,8192]{1,0:T(8,128)} %param.6) | copy-start | bytes 1572868
  38.9 9.2 %collective-permute-start.6 = (bf16[128,4096]{1,0:T(8,128)(2,1)S(1)}, bf16[128,4096]{1,0:T(8,128)(2,1)S(1)}, u32[]{:S(2)}, u32[]{:S(2)}) collective-permute-start(bf16[128,4096]{1,0:T(8,128)(2,1)S(1)} %project_send.1), channel_id=1, source_target_pairs={{0,1},{1,0},{2,3},{3,2},{4,5},{5,4},{6,7},{7,6},{8,9},{9,8},{10,11... | collective-permute-start | bytes 3145736 | tf_op jit(solution)/shard_map/ppermute | solution.py:202
  39.1 20.8 %copy-start.3 = (f32[16,8192]{1,0:T(8,128)S(1)}, f32[16,8192]{1,0:T(8,128)}, u32[]{:S(2)}) copy-start(f32[16,8192]{1,0:T(8,128)} %param.5) | copy-start | bytes 1572868
  48.4 11.5 %collective-permute-start.7 = (bf16[32,4096]{1,0:T(8,128)(2,1)S(1)}, bf16[32,4096]{1,0:T(8,128)(2,1)S(1)}, u32[]{:S(2)}, u32[]{:S(2)}) collective-permute-start(bf16[32,4096]{1,0:T(8,128)(2,1)S(1)} %get-tuple-element.24), channel_id=1, source_target_pairs={{0,2},{1,3},{2,0},{3,1},{4,6},{5,7},{6,4},{7,5},{8,10},{9,11},{10,... | collective-permute-start | bytes 786440 | tf_op jit(solution)/shard_map/ppermute | solution.py:180
  50.0 20.3 %collective-permute-start.8 = (bf16[32,4096]{1,0:T(8,128)(2,1)S(1)}, bf16[32,4096]{1,0:T(8,128)(2,1)S(1)}, u32[]{:S(2)}, u32[]{:S(2)}) collective-permute-start(bf16[32,4096]{1,0:T(8,128)(2,1)S(1)} %get-tuple-element.25), channel_id=1, source_target_pairs={{0,4},{1,5},{2,6},{3,7},{4,0},{5,1},{6,2},{7,3},{8,12},{9,13},{10,... | collective-permute-start | bytes 786440 | tf_op jit(solution)/shard_map/ppermute | solution.py:180
  58.5 13.7 %collective-permute-start.9 = (bf16[32,4096]{1,0:T(8,128)(2,1)S(1)}, bf16[32,4096]{1,0:T(8,128)(2,1)S(1)}, u32[]{:S(2)}, u32[]{:S(2)}) collective-permute-start(bf16[32,4096]{1,0:T(8,128)(2,1)S(1)} %get-tuple-element.26), channel_id=1, source_target_pairs={{0,6},{1,7},{2,4},{3,5},{4,2},{5,3},{6,0},{7,1},{8,14},{9,15},{10,... | collective-permute-start | bytes 786440 | tf_op jit(solution)/shard_map/ppermute | solution.py:180
  72.3 8.2 %collective-permute-start.11 = (bf16[32,4096]{1,0:T(8,128)(2,1)S(1)}, bf16[32,4096]{1,0:T(8,128)(2,1)S(1)}, u32[]{:S(2)}, u32[]{:S(2)}) collective-permute-start(bf16[32,4096]{1,0:T(8,128)(2,1)S(1)} %fusion.1), channel_id=1, source_target_pairs={{0,0},{1,1},{2,8},{3,9},{4,16},{5,17},{6,24},{7,25},{8,2},{9,3},{1... | collective-permute-start | bytes 786440 | tf_op jit(solution)/shard_map/ppermute | solution.py:184
  73.0 10.1 %collective-permute-start.12 = (bf16[32,4096]{1,0:T(8,128)(2,1)S(1)}, bf16[32,4096]{1,0:T(8,128)(2,1)S(1)}, u32[]{:S(2)}, u32[]{:S(2)}) collective-permute-start(bf16[32,4096]{1,0:T(8,128)(2,1)S(1)} %fusion.1), channel_id=1, source_target_pairs={{0,8},{1,9},{2,0},{3,1},{4,24},{5,25},{6,16},{7,17},{8,10},{9,11},... | collective-permute-start | bytes 786440 | tf_op jit(solution)/shard_map/ppermute | solution.py:184
  76.3 15.3 %collective-permute-start.13 = (bf16[32,4096]{1,0:T(8,128)(2,1)S(1)}, bf16[32,4096]{1,0:T(8,128)(2,1)S(1)}, u32[]{:S(2)}, u32[]{:S(2)}) collective-permute-start(bf16[32,4096]{1,0:T(8,128)(2,1)S(1)} %fusion.1), channel_id=1, source_target_pairs={{0,16},{1,17},{2,24},{3,25},{4,0},{5,1},{6,8},{7,9},{8,18},{9,19},... | collective-permute-start | bytes 786440 | tf_op jit(solution)/shard_map/ppermute | solution.py:184
  79.0 13.8 %collective-permute-start.14 = (bf16[32,4096]{1,0:T(8,128)(2,1)S(1)}, bf16[32,4096]{1,0:T(8,128)(2,1)S(1)}, u32[]{:S(2)}, u32[]{:S(2)}) collective-permute-start(bf16[32,4096]{1,0:T(8,128)(2,1)S(1)} %fusion.1), channel_id=1, source_target_pairs={{0,24},{1,25},{2,16},{3,17},{4,8},{5,9},{6,0},{7,1},{8,26},{9,27},... | collective-permute-start | bytes 786440 | tf_op jit(solution)/shard_map/ppermute | solution.py:184
  92.7 3.4 %copy-start.1 = (bf16[512,8192]{1,0:T(8,128)(2,1)S(1)}, bf16[512,8192]{1,0:T(8,128)(2,1)}, u32[]{:S(2)}) copy-start(bf16[512,8192]{1,0:T(8,128)(2,1)} %copy-done) | copy-start | bytes 25165828
  113.2 2.7 %collective-permute-start.15 = (bf16[64,8192]{1,0:T(8,128)(2,1)S(1)}, bf16[64,8192]{1,0:T(8,128)(2,1)S(1)}, u32[]{:S(2)}, u32[]{:S(2)}) collective-permute-start(bf16[64,8192]{1,0:T(8,128)(2,1)S(1)} %get-tuple-element.28), channel_id=1, source_target_pairs={{0,1},{1,0},{2,3},{3,2},{4,5},{5,4},{6,7},{7,6},{8,9},{9,8},{10,11... | collective-permute-start | bytes 3145736 | tf_op jit(solution)/shard_map/ppermute | solution.py:226
  116.1 13.4 %collective-permute-start.16 = (bf16[16,8192]{1,0:T(8,128)(2,1)S(1)}, bf16[16,8192]{1,0:T(8,128)(2,1)S(1)}, u32[]{:S(2)}, u32[]{:S(2)}) collective-permute-start(bf16[16,8192]{1,0:T(8,128)(2,1)S(1)} %get-tuple-element.30), channel_id=1, source_target_pairs={{0,2},{1,3},{2,0},{3,1},{4,6},{5,7},{6,4},{7,5},{8,10},{9,11},{10,... | collective-permute-start | bytes 786440 | tf_op jit(solution)/shard_map/ppermute | solution.py:180
  118.1 21.5 %collective-permute-start.17 = (bf16[16,8192]{1,0:T(8,128)(2,1)S(1)}, bf16[16,8192]{1,0:T(8,128)(2,1)S(1)}, u32[]{:S(2)}, u32[]{:S(2)}) collective-permute-start(bf16[16,8192]{1,0:T(8,128)(2,1)S(1)} %get-tuple-element.31), channel_id=1, source_target_pairs={{0,4},{1,5},{2,6},{3,7},{4,0},{5,1},{6,2},{7,3},{8,12},{9,13},{10,... | collective-permute-start | bytes 786440 | tf_op jit(solution)/shard_map/ppermute | solution.py:180
  128.1 13.3 %collective-permute-start.18 = (bf16[16,8192]{1,0:T(8,128)(2,1)S(1)}, bf16[16,8192]{1,0:T(8,128)(2,1)S(1)}, u32[]{:S(2)}, u32[]{:S(2)}) collective-permute-start(bf16[16,8192]{1,0:T(8,128)(2,1)S(1)} %get-tuple-element.32), channel_id=1, source_target_pairs={{0,6},{1,7},{2,4},{3,5},{4,2},{5,3},{6,0},{7,1},{8,14},{9,15},{10,... | collective-permute-start | bytes 786440 | tf_op jit(solution)/shard_map/ppermute | solution.py:180

commit v2 on v0

v2 whole, which is shorter than its diff:
```python
import jax
import jax.numpy as jnp
from jax import lax
from jax.experimental import pallas as pl
from jax.experimental.pallas import tpu as pltpu
from jax.sharding import PartitionSpec as P

ITERS = 2
CORES = 2
CHUNKS = 2
TILE = 512
PIECE_ROWS = 256
SOON_ROWS = 1024
LIMIT_BYTES = 6144 << 10
STREAM_LIMIT_BYTES = 8192 << 10
HELD_BYTES = 36 << 20
BUFFERS = 3

VMEM = pl.BlockSpec(memory_space=pltpu.VMEM)
HBM = pl.BlockSpec(memory_space=pl.ANY)


def place():
    lane = lax.axis_index("col")
    return lax.axis_index("row"), lane // CORES, lax.rem(lane, CORES)


def call(kernel, args, in_specs, outs, scratch, name, flops, moved, limit=LIMIT_BYTES):
    return pl.pallas_call(
        kernel,
        in_specs=in_specs,
        out_specs=[VMEM] * len(outs),
        out_shape=outs,
        scratch_shapes=scratch,
        compiler_params=pltpu.CompilerParams(vmem_limit_bytes=limit),
        cost_estimate=pl.CostEstimate(flops=flops, bytes_accessed=moved, transcendentals=0),
        name=name,
    )(*args)


def shape(rows, cols, dtype=jnp.bfloat16):
    return jax.ShapeDtypeStruct((rows, cols), dtype)


def hold(cycle, start, rows, after):
    cols = cycle.shape[1]
    piece = min(PIECE_ROWS, rows)
    count = rows // piece

    def kernel(cycle_ref, after_ref, *refs):
        copies = [
            pltpu.make_async_copy(
                cycle_ref.at[pl.ds(start + index * piece, piece)], refs[index], refs[count + 1].at[index]
            )
            for index in range(count)
        ]
        for copy in copies:
            copy.start()
        for copy in copies:
            copy.wait()
        refs[count][...] = jnp.zeros_like(refs[count])

    return call(
        kernel, [cycle, after], [HBM, HBM],
        [pltpu.VMEM((piece, cols), cycle.dtype)] * count + [shape(8, 128, jnp.float32)],
        [pltpu.SemaphoreType.DMA((count,))], "hold", 0, 2 * rows * cols * 2, 1 << 20,
    )


def gather_rows(block_refs, lhs):
    rows = block_refs[0].shape[0]
    for index, ref in enumerate(block_refs):
        lhs[index * rows : (index + 1) * rows, :] = ref[...]


def stream_dot(blocks, cycle, held, columns, width, name):
    count, pieces, parts = len(blocks), len(held), len(columns)
    block_rows, depth = blocks[0].shape
    piece = held[0].shape[0] if held else 0
    streamed = depth - pieces * piece
    tile = min(TILE, width)
    steps = width // tile
    rows = count * block_rows

    def kernel(*refs):
        held_refs, cycle_ref = refs[count : count + pieces], refs[count + pieces]
        out_refs = refs[count + pieces + 1 : count + pieces + 1 + parts]
        lhs, buffer, sems = refs[count + pieces + 1 + parts :]

        def column_of(n, step):
            return pl.ds(pl.multiple_of(columns[n](step * tile), tile), tile)

        def fetch(n, step):
            slot = (n * steps + step) % BUFFERS
            return pltpu.make_async_copy(
                cycle_ref.at[pl.ds(0, streamed), column_of(n, step)], buffer.at[slot], sems.at[slot]
            )

        order = [(n, step) for n in range(parts) for step in range(steps)]
        for at in order[:BUFFERS]:
            fetch(*at).start()
        gather_rows(refs[:count], lhs)
        for index, (n, step) in enumerate(order):
            fetch(n, step).wait()
            total = jnp.dot(lhs[:, :streamed], buffer[index % BUFFERS], preferred_element_type=jnp.float32)
            if index + BUFFERS < len(order):
                fetch(*order[index + BUFFERS]).start()
            for k, held_ref in enumerate(held_refs):
                at = streamed + k * piece
                total += jnp.dot(
                    lhs[:, at : at + piece], held_ref[:, column_of(n, step)], preferred_element_type=jnp.float32
                )
            out_refs[n][:, step * tile : (step + 1) * tile] = total

    return call(
        kernel, [*blocks, *held, cycle], [VMEM] * (count + pieces) + [HBM],
        [pltpu.VMEM((rows, width), jnp.float32)] * parts,
        [
            pltpu.VMEM((rows, depth), jnp.bfloat16),
            pltpu.VMEM((BUFFERS, streamed, tile), jnp.bfloat16),
            pltpu.SemaphoreType.DMA((BUFFERS,)),
        ],
        name, 2 * rows * depth * width * parts, 2 * streamed * width * parts, STREAM_LIMIT_BYTES,
    )


def held_dot(blocks, held, partial, column_of, store, outs, name):
    count, pieces = len(blocks), len(held)
    block_rows, depth = blocks[0].shape
    rows, width = partial.shape
    piece = held[0].shape[0]
    tile = min(TILE, width)
    steps = width // tile

    def kernel(*refs):
        held_refs, partial_ref = refs[count : count + pieces], refs[count + pieces]
        out_refs, lhs = refs[count + pieces + 1 : -1], refs[-1]
        gather_rows(refs[:count], lhs)
        for step in range(steps):
            total = partial_ref[:, step * tile : (step + 1) * tile]
            for index, held_ref in enumerate(held_refs):
                total += jnp.dot(
                    lhs[:, index * piece : (index + 1) * piece],
                    held_ref[:, pl.ds(pl.multiple_of(column_of(step * tile), tile), tile)],
                    preferred_element_type=jnp.float32,
                )
            store(total, step * tile, tile, out_refs)

    return call(
        kernel, [*blocks, *held, partial], [VMEM] * (count + pieces + 1), outs,
        [pltpu.VMEM((rows, depth), jnp.bfloat16)], name, 2 * rows * depth * width, 0,
    )


def add_split(keep, received, count, name):
    rows, width = keep.shape
    block_rows = rows // count

    def kernel(keep_ref, received_ref, *out_refs):
        for k in range(count):
            at = slice(k * block_rows, (k + 1) * block_rows)
            total = keep_ref[at, :] + received_ref[at, :].astype(jnp.float32)
            out_refs[k][...] = total.astype(out_refs[k].dtype)

    outs = [shape(block_rows, width, jnp.float32)] + [shape(block_rows, width)] * (count - 1)
    return call(kernel, [keep, received], [VMEM] * 2, outs, [], name, rows * width, 8 * rows * width)


def pick(planes, after, name):
    count = len(planes)

    def kernel(*refs):
        z, p, _ = place()
        for k in range(count):
            for source in range(count):
                @pl.when((z ^ p ^ k) == source)
                def _():
                    refs[count + len(after) + k][...] = refs[source][...]

    size = planes[0].size
    return call(
        kernel, [*planes, *after], [VMEM] * count + [HBM] * len(after), [shape(*planes[0].shape)] * count, [], name, 0, 4 * count * size
    )


def shards(multipliers, source, denominator, cycle):
    planes, lanes = lax.axis_size("row"), lax.axis_size("col")
    chips = lanes // CORES
    local_rows, local_cols = multipliers.shape
    half = local_cols // CORES
    part = half // CHUNKS
    wide = local_cols // CHUNKS
    block_rows = local_rows * CORES
    total_rows = local_rows * lanes

    first = place()[2] == 0
    core_swap = [(i, i ^ 1) for i in range(lanes)]
    chip_swap = [[(i, i ^ (k * CORES)) for i in range(lanes)] for k in range(chips)]
    plane_swap = [[(i, i ^ k) for i in range(planes)] for k in range(planes)]

    def pair(array):
        low, high = array[:, :half], array[:, half:]
        mine = jnp.where(first, low, high)
        theirs = lax.ppermute(jnp.where(first, high, low), "col", core_swap)
        top, bottom = jnp.where(first, mine, theirs), jnp.where(first, theirs, mine)
        return [
            jnp.concatenate([top[:, n * part : (n + 1) * part], bottom[:, n * part : (n + 1) * part]], axis=0)
            for n in range(CHUNKS)
        ]

    far = planes // 2

    def set_out(chunk):
        return {0: chunk, far: lax.ppermute(chunk, "row", plane_swap[far]), 1: lax.ppermute(chunk, "row", plane_swap[1])}

    def go_on(seen):
        for k in range(1, planes):
            low = k & -k
            if k not in seen:
                seen[k] = lax.ppermute(seen[k ^ low], "row", plane_swap[low])

    def tie(*arrays):
        return lax.optimization_barrier(arrays)

    def deal(seen, after=()):
        picked = pick([seen[k] for k in range(planes)], after, "pick")
        return [picked[0]] + [lax.ppermute(picked[k], "col", chip_swap[k]) for k in range(1, chips)]

    def scatter_add(keep, received, name):
        own, *others = add_split(keep, received, chips, name)
        for k in range(1, chips):
            own = own + lax.ppermute(others[k - 1], "col", chip_swap[k]).astype(jnp.float32)
        return own

    def column_in_halves(n):
        def column_of(at):
            core = place()[2]
            away = at < part
            return jnp.where(away, (1 - core) * half + n * part + at, core * half + n * part + at - part)

        return column_of

    def column_in_order(n):
        return lambda at: n * wide + at

    def store_halves(total, at, tile, out_refs):
        if at < part:
            out_refs[0][:, at : at + tile] = total.astype(jnp.bfloat16)
        else:
            out_refs[1][:, at - part : at - part + tile] = total

    def store_rows(total, at, tile, out_refs):
        mine = place()[2] == 0
        for index in range(chips):
            row = index * block_rows
            low, high = total[row : row + local_rows], total[row + local_rows : row + block_rows]
            to = slice(index * local_rows, (index + 1) * local_rows)
            out_refs[0][to, at : at + tile] = jnp.where(mine, high, low).astype(jnp.bfloat16)
            out_refs[1][to, at : at + tile] = jnp.where(mine, low, high)

    current = pair(multipliers)
    budget = HELD_BYTES // (2 * local_cols)
    streamed = min(part, max(PIECE_ROWS, cycle.shape[0] - budget))
    early = (part - streamed) // PIECE_ROWS
    held_rows = cycle.shape[0] - streamed
    soon = min(SOON_ROWS, held_rows - PIECE_ROWS)

    for sweep in range(ITERS):
        last = sweep == ITERS - 1
        columns = column_in_order if last else column_in_halves
        here, later = current
        seen, done = set_out(here), []
        if sweep == 0:
            *held, token = hold(cycle, streamed, soon, here)
            done = [token]
        later, seen[far], seen[1], *done = tie(later, seen[far], seen[1], *done)
        seen_later = set_out(later)
        if sweep == 0:
            *more, token = hold(cycle, streamed + soon, held_rows - soon, seen[far])
            held += more
            seen_later[far], token = tie(seen_later[far], token)
            source, denominator, token = tie(source, denominator, token)
            source_pair, denominator_pair = pair(source), pair(denominator)
            done.append(token)
        go_on(seen)
        go_on(seen_later)
        blocks = [deal(seen), deal(seen_later, done)]
        partial = stream_dot(
            blocks[0], cycle, held[:early], [columns(n) for n in range(CHUNKS)], wide, "stream_dot"
        )
        current = []
        for n in range(CHUNKS):
            if last:
                rows, width, store = total_rows // CORES, wide, store_rows
                src, den = source[:, n * wide : (n + 1) * wide], denominator[:, n * wide : (n + 1) * wide]
            else:
                rows, width, store = total_rows, part, store_halves
                src, den = source_pair[n], denominator_pair[n]
            send, keep = held_dot(
                blocks[1], held[early:], partial[n], columns(n), store,
                [shape(rows, width), shape(rows, width, jnp.float32)], "held_dot",
            )
            received = lax.ppermute(send, "col", core_swap)
            product = scatter_add(keep, received, "add_split")
            current.append(((src + product) / den).astype(jnp.bfloat16))
    return jnp.concatenate(current, axis=1)


def solution(mesh):
    placed = (P("col", "row"), P("col", "row"), P("col", "row"), P("col", "row"))
    return jax.shard_map(
        shards, mesh=mesh, in_specs=placed, out_specs=P("col", "row"), check_vma=False
    )
```

time: 245 us -> 128 us (0.52)
  waiting for transfers between devices: 139 us -> 27 us
  starting transfers between devices: 0.13 us -> 49.8 us
  matrix products: 48.6 us -> 0 us
  Pallas kernels: 0 us -> 47.5 us
  blocking collectives: 37.6 us -> 0 us
  between operations: 13.1 us -> 0.39 us
  local copies, waits for them, and re-layouts: 2.59 us -> 0.1 us
    reduce_scatter x2 -> x0, waiting for transfers between devices: 78.1 us -> none  [shards(): lax.psum_scatter(project_rows(jnp.int32(0), local_rows * lax.axis_size('c...]
    all_gather x2 -> x0, waiting for transfers between devices: 60.3 us -> none  [realign(): gathered = lax.all_gather(current, 'row', axis=1, tiled=True)]
    ppermute x0 -> x43, starting transfers between devices: none -> 49.8 us  [the longest x12 17.2 us: scatter_add(): lax.ppermute(others[k - 1], 'col', chip_swap[k]).astype(jnp.float32)]
    dot_general x2 -> x0, matrix products: 48.6 us -> none  [project_rows(): return jnp.dot(aligned, cycle, preferred_element_type=jnp.float32)]
    pallas_call x0 -> x16, Pallas kernels: none -> 47.5 us  [call(): pl.pallas_call(kernel, in_specs=in_specs, out_specs=[VMEM] * len(outs), o...]
    all_to_all x2 -> x0, blocking collectives: 37.6 us -> none  [realign(): lax.all_to_all(gathered, 'col', split_axis=1, concat_axis=0, tiled=True)]
    ppermute x0 -> x43, waiting for transfers between devices: none -> 27 us  [the longest x12 9.85 us: scatter_add(): lax.ppermute(others[k - 1], 'col', chip_swap[k]).astype(jnp.float32)]
    convert_element_type x2 -> x3, other arithmetic: 3.47 us -> 0.4 us  [shards(): current.append(((src + product) / den).astype(jnp.bfloat16))]
  transfers between devices with their start and end apart: 4 -> 43, of which waited for: 4 -> 16; matrix products, arithmetic and copies ran while one was open for 0% -> 0% of each run, Pallas kernels for 0% -> 35%
where the time goes in v2:
time: 128 us
  starting transfers between devices  49.8 us (39%)
  Pallas kernels  47.5 us (37%)
  waiting for transfers between devices  27 us (21%)
  other arithmetic  3.28 us (3%)
    pallas_call x16, Pallas kernels, call(): pl.pallas_call(kernel, in_specs=in_specs, out_specs=[VMEM] * len(outs), o...  47.5 us
    ppermute x12, starting transfers between devices, scatter_add(): lax.ppermute(others[k - 1], 'col', chip_swap[k]).astype(jnp.float32)  17.2 us
    ppermute x12, starting transfers between devices, deal(): lax.ppermute(picked[k], 'col', chip_swap[k])  15.7 us
    ppermute x12, waiting for transfers between devices, scatter_add(): lax.ppermute(others[k - 1], 'col', chip_swap[k]).astype(jnp.float32)  9.85 us
    ppermute x4, waiting for transfers between devices, set_out(): lax.ppermute(chunk, 'row', plane_swap[far])  9.58 us
    ppermute x4, starting transfers between devices, set_out(): lax.ppermute(chunk, 'row', plane_swap[1])  5.63 us
    ppermute x4, starting transfers between devices, set_out(): lax.ppermute(chunk, 'row', plane_swap[far])  5.54 us
    ppermute x4, waiting for transfers between devices, go_on(): seen[k] = lax.ppermute(seen[k ^ low], 'row', plane_swap[low])  4.21 us
  transfers between devices with their start and end apart: 43, of which 16 were waited for; matrix products, arithmetic and copies ran while one was open for 0% of the time, Pallas kernels for 35%

profile of v2, /device:TPU:0, one launch (start us, length us, event | category | flops | bytes accessed | tf_op | source)
XLA Modules:
  0.0 128.1 jit_solution(9088593003744464558)
XLA Ops:
  0.0 1.0 broadcast_select_fusion.6
  1.0 0.5 collective-permute-start
  1.5 1.0 collective-permute-done
  2.5 1.0 broadcast_select_fusion.5
  3.5 3.0 %collective-permute-start.2 = (bf16[32,2048]{1,0:T(8,128)(2,1)S(1)}, bf16[32,2048]{1,0:T(8,128)(2,1)S(1)}, u32[]{:S(2)}, u32[]{:S(2)}) collective-permute-start(bf16[32,2048]{1,0:T(8,128)(2,1)S(1)} %pad_maximum_fusion.2.after_ref.refs_0_), channel_id=1, source_target_pairs={{0,8},{8,0},{16,24},{24,16},{1,9},{9,1},{17,25},{25,17},{2,10},{10... | collective-permute-start | bytes 393224 | tf_op jit(solution)/shard_map/ppermute | solution.py:214
  6.5 2.6 %collective-permute-start.1 = (bf16[32,2048]{1,0:T(8,128)(2,1)S(1)}, bf16[32,2048]{1,0:T(8,128)(2,1)S(1)}, u32[]{:S(2)}, u32[]{:S(2)}) collective-permute-start(bf16[32,2048]{1,0:T(8,128)(2,1)S(1)} %pad_maximum_fusion.2.after_ref.refs_0_), channel_id=1, source_target_pairs={{0,16},{8,24},{16,0},{24,8},{1,17},{9,25},{17,1},{25,9},{2,18},{10... | collective-permute-start | bytes 393224 | tf_op jit(solution)/shard_map/ppermute | solution.py:214
  9.1 5.9 %hold.2 = (bf16[256,8192]{1,0:T(8,128)(2,1)S(1)}, bf16[256,8192]{1,0:T(8,128)(2,1)S(1)}, bf16[256,8192]{1,0:T(8,128)(2,1)S(1)}, bf16[256,8192]{1,0:T(8,128)(2,1)S(1)}, f32[8,128]{1,0:T(8,128)S(1)}) custom-call(bf16[4096,8192]{1,0:T(8,128)(2,1)} %refs_5_.3, bf16[32,2048]{1,0:T(8,128)(2,1)S(1)} %pad_maximum_fusion.2.after_ref.refs_0_), custom_call_target="tpu_custom_call" | custom-call | bytes 33554432 | tf_op jit(solution)/shard_map/hold/pallas_call | solution.py:29
  15.1 0.5 collective-permute-done.1.after_ref.refs_2_
  15.6 0.4 collective-permute-start.10
  16.0 2.6 %collective-permute-start.3 = (bf16[32,2048]{1,0:T(8,128)(2,1)S(1)}, bf16[32,2048]{1,0:T(8,128)(2,1)S(1)}, u32[]{:S(2)}, u32[]{:S(2)}) collective-permute-start(bf16[32,2048]{1,0:T(8,128)(2,1)S(1)} %pad_maximum_fusion.1.refs_0_), channel_id=1, source_target_pairs={{0,16},{8,24},{16,0},{24,8},{1,17},{9,25},{17,1},{25,9},{2,18},{10... | collective-permute-start | bytes 393224 | tf_op jit(solution)/shard_map/ppermute | solution.py:214
  18.7 7.1 %hold.3 = (bf16[256,8192]{1,0:T(8,128)(2,1)S(1)}, bf16[256,8192]{1,0:T(8,128)(2,1)S(1)}, bf16[256,8192]{1,0:T(8,128)(2,1)S(1)}, bf16[256,8192]{1,0:T(8,128)(2,1)...) custom-call(bf16[4096,8192]{1,0:T(8,128)(2,1)} %refs_5_.3, ...), custom_call_target="tpu_custom_call" | custom-call | bytes 41943040 | tf_op jit(solution)/shard_map/hold/pallas_call | solution.py:29
  25.9 1.6 %collective-permute-start.11 = (bf16[32,2048]{1,0:T(8,128)(2,1)S(1)}, bf16[32,2048]{1,0:T(8,128)(2,1)S(1)}, u32[]{:S(2)}, u32[]{:S(2)}) collective-permute-start(bf16[32,2048]{1,0:T(8,128)(2,1)S(1)} %get-tuple-element.95), channel_id=1, source_target_pairs={{0,2},{1,3},{2,0},{3,1},{4,6},{5,7},{6,4},{7,5},{8,10},{9,11},{10,... | collective-permute-start | bytes 393224 | tf_op jit(solution)/shard_map/ppermute | solution.py:227
  27.5 1.5 %collective-permute-start.12 = (bf16[32,2048]{1,0:T(8,128)(2,1)S(1)}, bf16[32,2048]{1,0:T(8,128)(2,1)S(1)}, u32[]{:S(2)}, u32[]{:S(2)}) collective-permute-start(bf16[32,2048]{1,0:T(8,128)(2,1)S(1)} %get-tuple-element.96), channel_id=1, source_target_pairs={{0,4},{1,5},{2,6},{3,7},{4,0},{5,1},{6,2},{7,3},{8,12},{9,13},{10,... | collective-permute-start | bytes 393224 | tf_op jit(solution)/shard_map/ppermute | solution.py:227
  29.0 0.5 collective-permute-start.13
  29.5 2.0 %collective-permute-start.6 = (bf16[32,2048]{1,0:T(8,128)(2,1)S(1)}, bf16[32,2048]{1,0:T(8,128)(2,1)S(1)}, u32[]{:S(2)}, u32[]{:S(2)}) collective-permute-start(bf16[32,2048]{1,0:T(8,128)(2,1)S(1)} %collective-permute-done.3.refs_2_), channel_id=1, source_target_pairs={{0,8},{8,0},{16,24},{24,16},{1,9},{9,1},{17,25},{25,17},{2,10},{10... | collective-permute-start | bytes 393224 | tf_op jit(solution)/shard_map/ppermute | solution.py:220
  31.6 2.8 %collective-permute-done.6.refs_3_ = bf16[32,2048]{1,0:T(8,128)(2,1)S(1)} collective-permute-done((bf16[32,2048]{1,0:T(8,128)(2,1)S(1)}, bf16[32,2048]{1,0:T(8,128)(2,1)S(1)}, u32[]{:S(2)}, u32[]{:S(2)}) %collective-permute-start.6) | collective-permute-done | bytes 131104 | tf_op jit(solution)/shard_map/ppermute | solution.py:220
  34.5 1.6 %collective-permute-start.7 = (bf16[32,2048]{1,0:T(8,128)(2,1)S(1)}, bf16[32,2048]{1,0:T(8,128)(2,1)S(1)}, u32[]{:S(2)}, u32[]{:S(2)}) collective-permute-start(bf16[32,2048]{1,0:T(8,128)(2,1)S(1)} %get-tuple-element.82), channel_id=1, source_target_pairs={{0,2},{1,3},{2,0},{3,1},{4,6},{5,7},{6,4},{7,5},{8,10},{9,11},{10,... | collective-permute-start | bytes 393224 | tf_op jit(solution)/shard_map/ppermute | solution.py:227
  36.1 1.5 %collective-permute-start.8 = (bf16[32,2048]{1,0:T(8,128)(2,1)S(1)}, bf16[32,2048]{1,0:T(8,128)(2,1)S(1)}, u32[]{:S(2)}, u32[]{:S(2)}) collective-permute-start(bf16[32,2048]{1,0:T(8,128)(2,1)S(1)} %get-tuple-element.83), channel_id=1, source_target_pairs={{0,4},{1,5},{2,6},{3,7},{4,0},{5,1},{6,2},{7,3},{8,12},{9,13},{10,... | collective-permute-start | bytes 393224 | tf_op jit(solution)/shard_map/ppermute | solution.py:227
  37.6 0.5 collective-permute-start.9
  38.1 11.9 %stream_dot.2 = (f32[128,4096]{1,0:T(8,128)S(1)}, f32[128,4096]{1,0:T(8,128)S(1)}) custom-call(bf16[32,2048]{1,0:T(8,128)(2,1)S(1)} %get-tuple-element.94.refs_0_, bf16[32,2048]{1,0:T(8,128)(2,1)S(1)} %collective-permute-done.11.refs_1_, bf16[32,2048]{1,0:T(8,128)(2,1)S(1)} %collective-permute-done.12.refs_2_, ...), custom_call_target="tpu_custom_call" | custom-call | flops 4294967296 | bytes 29360128 | tf_op jit(solution)/shard_map/stream_dot/pallas_call | solution.py:29
  50.2 2.5 %held_dot.5 = (bf16[128,2048]{1,0:T(8,128)(2,1)S(1)}, f32[128,2048]{1,0:T(8,128)S(1)}) custom-call(bf16[32,2048]{1,0:T(8,128)(2,1)S(1)} %get-tuple-element.81.refs_0_, bf16[32,2048]{1,0:T(8,128)(2,1)S(1)} %collective-permute-done.7.refs_1_, bf16[32,2048]{1,0:T(8,128)(2,1)S(1)} %collective-permute-done.8.refs_2_, ...), custom_call_target="tpu_custom_call" | custom-call | flops 2147483648 | tf_op jit(solution)/shard_map/held_dot/pallas_call | solution.py:29
  52.7 2.5 %held_dot.4 = (bf16[128,2048]{1,0:T(8,128)(2,1)S(1)}, f32[128,2048]{1,0:T(8,128)S(1)}) custom-call(bf16[32,2048]{1,0:T(8,128)(2,1)S(1)} %get-tuple-element.81.refs_0_, bf16[32,2048]{1,0:T(8,128)(2,1)S(1)} %collective-permute-done.7.refs_1_, bf16[32,2048]{1,0:T(8,128)(2,1)S(1)} %collective-permute-done.8.refs_2_, ...), custom_call_target="tpu_custom_call" | custom-call | flops 2147483648 | tf_op jit(solution)/shard_map/held_dot/pallas_call | solution.py:29
  55.2 0.6 collective-permute-start.14
  56.0 1.5 %collective-permute-start.20 = (bf16[32,2048]{1,0:T(8,128)(2,1)S(1)}, bf16[32,2048]{1,0:T(8,128)(2,1)S(1)}, u32[]{:S(2)}, u32[]{:S(2)}) collective-permute-start(bf16[32,2048]{1,0:T(8,128)(2,1)S(1)} %get-tuple-element.111), channel_id=1, source_target_pairs={{0,2},{1,3},{2,0},{3,1},{4,6},{5,7},{6,4},{7,5},{8,10},{9,11},{10,... | collective-permute-start | bytes 393224 | tf_op jit(solution)/shard_map/ppermute | solution.py:232
  57.5 1.5 %collective-permute-start.21 = (bf16[32,2048]{1,0:T(8,128)(2,1)S(1)}, bf16[32,2048]{1,0:T(8,128)(2,1)S(1)}, u32[]{:S(2)}, u32[]{:S(2)}) collective-permute-start(bf16[32,2048]{1,0:T(8,128)(2,1)S(1)} %get-tuple-element.112), channel_id=1, source_target_pairs={{0,4},{1,5},{2,6},{3,7},{4,0},{5,1},{6,2},{7,3},{8,12},{9,13},{10,... | collective-permute-start | bytes 393224 | tf_op jit(solution)/shard_map/ppermute | solution.py:232
  59.0 0.5 collective-permute-start.22
  59.7 1.5 %collective-permute-start.15 = (bf16[32,2048]{1,0:T(8,128)(2,1)S(1)}, bf16[32,2048]{1,0:T(8,128)(2,1)S(1)}, u32[]{:S(2)}, u32[]{:S(2)}) collective-permute-start(bf16[32,2048]{1,0:T(8,128)(2,1)S(1)} %get-tuple-element.103), channel_id=1, source_target_pairs={{0,2},{1,3},{2,0},{3,1},{4,6},{5,7},{6,4},{7,5},{8,10},{9,11},{10,... | collective-permute-start | bytes 393224 | tf_op jit(solution)/shard_map/ppermute | solution.py:232
  61.2 1.5 %collective-permute-start.16 = (bf16[32,2048]{1,0:T(8,128)(2,1)S(1)}, bf16[32,2048]{1,0:T(8,128)(2,1)S(1)}, u32[]{:S(2)}, u32[]{:S(2)}) collective-permute-start(bf16[32,2048]{1,0:T(8,128)(2,1)S(1)} %get-tuple-element.104), channel_id=1, source_target_pairs={{0,4},{1,5},{2,6},{3,7},{4,0},{5,1},{6,2},{7,3},{8,12},{9,13},{10,... | collective-permute-start | bytes 393224 | tf_op jit(solution)/shard_map/ppermute | solution.py:232
  62.7 2.1 %collective-permute-start.17 = (bf16[32,2048]{1,0:T(8,128)(2,1)S(1)}, bf16[32,2048]{1,0:T(8,128)(2,1)S(1)}, u32[]{:S(2)}, u32[]{:S(2)}) collective-permute-start(bf16[32,2048]{1,0:T(8,128)(2,1)S(1)} %get-tuple-element.105), channel_id=1, source_target_pairs={{0,6},{1,7},{2,4},{3,5},{4,2},{5,3},{6,0},{7,1},{8,14},{9,15},{10,... | collective-permute-start | bytes 393224 | tf_op jit(solution)/shard_map/ppermute | solution.py:232
  64.8 1.0 collective-permute-done.21
  65.9 0.5 collective-permute-done.22
  66.5 2.0 %collective-permute-start.24 = (bf16[32,2048]{1,0:T(8,128)(2,1)S(1)}, bf16[32,2048]{1,0:T(8,128)(2,1)S(1)}, u32[]{:S(2)}, u32[]{:S(2)}) collective-permute-start(bf16[32,2048]{1,0:T(8,128)(2,1)S(1)} %fusion.3.refs_0_), channel_id=1, source_target_pairs={{0,8},{8,0},{16,24},{24,16},{1,9},{9,1},{17,25},{25,17},{2,10},{10... | collective-permute-start | bytes 393224 | tf_op jit(solution)/shard_map/ppermute | solution.py:214
  68.5 0.4 collective-permute-start.23
  68.9 2.2 %collective-permute-done.16 = bf16[32,2048]{1,0:T(8,128)(2,1)S(1)} collective-permute-done((bf16[32,2048]{1,0:T(8,128)(2,1)S(1)}, bf16[32,2048]{1,0:T(8,128)(2,1)S(1)}, u32[]{:S(2)}, u32[]{:S(2)}) %collective-permute-start.16) | collective-permute-done | bytes 131104 | tf_op jit(solution)/shard_map/ppermute | solution.py:232
  71.2 1.5 %collective-permute-done.24.refs_1_ = bf16[32,2048]{1,0:T(8,128)(2,1)S(1)} collective-permute-done((bf16[32,2048]{1,0:T(8,128)(2,1)S(1)}, bf16[32,2048]{1,0:T(8,128)(2,1)S(1)}, u32[]{:S(2)}, u32[]{:S(2)}) %collective-permute-start.24) | collective-permute-done | bytes 131104 | tf_op jit(solution)/shard_map/ppermute | solution.py:214
  72.7 5.0 %collective-permute-done.23.refs_2_ = bf16[32,2048]{1,0:T(8,128)(2,1)S(1)} collective-permute-done((bf16[32,2048]{1,0:T(8,128)(2,1)S(1)}, bf16[32,2048]{1,0:T(8,128)(2,1)S(1)}, u32[]{:S(2)}, u32[]{:S(2)}) %collective-permute-start.23) | collective-permute-done | bytes 131104 | tf_op jit(solution)/shard_map/ppermute | solution.py:214
  77.7 1.5 %collective-permute-start.31 = (bf16[32,2048]{1,0:T(8,128)(2,1)S(1)}, bf16[32,2048]{1,0:T(8,128)(2,1)S(1)}, u32[]{:S(2)}, u32[]{:S(2)}) collective-permute-start(bf16[32,2048]{1,0:T(8,128)(2,1)S(1)} %collective-permute-done.23.refs_2_), channel_id=1, source_target_pairs={{0,8},{8,0},{16,24},{24,16},{1,9},{9,1},{17,25},{25,17},{2,10},{10... | collective-permute-start | bytes 393224 | tf_op jit(solution)/shard_map/ppermute | solution.py:220
  79.2 0.6 collective-permute-start.25
  79.7 4.1 %collective-permute-done.26.refs_2_ = bf16[32,2048]{1,0:T(8,128)(2,1)S(1)} collective-permute-done((bf16[32,2048]{1,0:T(8,128)(2,1)S(1)}, bf16[32,2048]{1,0:T(8,128)(2,1)S(1)}, u32[]{:S(2)}, u32[]{:S(2)}) %collective-permute-start.26) | collective-permute-done | bytes 131104 | tf_op jit(solution)/shard_map/ppermute | solution.py:214
  83.8 1.4 %collective-permute-done.31.refs_3_ = bf16[32,2048]{1,0:T(8,128)(2,1)S(1)} collective-permute-done((bf16[32,2048]{1,0:T(8,128)(2,1)S(1)}, bf16[32,2048]{1,0:T(8,128)(2,1)S(1)}, u32[]{:S(2)}, u32[]{:S(2)}) %collective-permute-start.31) | collective-permute-done | bytes 131104 | tf_op jit(solution)/shard_map/ppermute | solution.py:220
  85.3 1.4 %collective-permute-start.32 = (bf16[32,2048]{1,0:T(8,128)(2,1)S(1)}, bf16[32,2048]{1,0:T(8,128)(2,1)S(1)}, u32[]{:S(2)}, u32[]{:S(2)}) collective-permute-start(bf16[32,2048]{1,0:T(8,128)(2,1)S(1)} %get-tuple-element.122), channel_id=1, source_target_pairs={{0,2},{1,3},{2,0},{3,1},{4,6},{5,7},{6,4},{7,5},{8,10},{9,11},{10,... | collective-permute-start | bytes 393224 | tf_op jit(solution)/shard_map/ppermute | solution.py:227
  86.7 1.5 %collective-permute-start.33 = (bf16[32,2048]{1,0:T(8,128)(2,1)S(1)}, bf16[32,2048]{1,0:T(8,128)(2,1)S(1)}, u32[]{:S(2)}, u32[]{:S(2)}) collective-permute-start(bf16[32,2048]{1,0:T(8,128)(2,1)S(1)} %get-tuple-element.123), channel_id=1, source_target_pairs={{0,4},{1,5},{2,6},{3,7},{4,0},{5,1},{6,2},{7,3},{8,12},{9,13},{10,... | collective-permute-start | bytes 393224 | tf_op jit(solution)/shard_map/ppermute | solution.py:227
  88.1 1.4 %collective-permute-start.34 = (bf16[32,2048]{1,0:T(8,128)(2,1)S(1)}, bf16[32,2048]{1,0:T(8,128)(2,1)S(1)}, u32[]{:S(2)}, u32[]{:S(2)}) collective-permute-start(bf16[32,2048]{1,0:T(8,128)(2,1)S(1)} %get-tuple-element.124), channel_id=1, source_target_pairs={{0,6},{1,7},{2,4},{3,5},{4,2},{5,3},{6,0},{7,1},{8,14},{9,15},{10,... | collective-permute-start | bytes 393224 | tf_op jit(solution)/shard_map/ppermute | solution.py:227
  89.5 0.3 pick.6
  89.8 0.7 collective-permute-start.28
  90.5 2.3 %collective-permute-start.29 = (bf16[32,2048]{1,0:T(8,128)(2,1)S(1)}, bf16[32,2048]{1,0:T(8,128)(2,1)S(1)}, u32[]{:S(2)}, u32[]{:S(2)}) collective-permute-start(bf16[32,2048]{1,0:T(8,128)(2,1)S(1)} %get-tuple-element.117), channel_id=1, source_target_pairs={{0,4},{1,5},{2,6},{3,7},{4,0},{5,1},{6,2},{7,3},{8,12},{9,13},{10,... | collective-permute-start | bytes 393224 | tf_op jit(solution)/shard_map/ppermute | solution.py:227
  92.8 1.4 %collective-permute-start.30 = (bf16[32,2048]{1,0:T(8,128)(2,1)S(1)}, bf16[32,2048]{1,0:T(8,128)(2,1)S(1)}, u32[]{:S(2)}, u32[]{:S(2)}) collective-permute-start(bf16[32,2048]{1,0:T(8,128)(2,1)S(1)} %get-tuple-element.118), channel_id=1, source_target_pairs={{0,6},{1,7},{2,4},{3,5},{4,2},{5,3},{6,0},{7,1},{8,14},{9,15},{10,... | collective-permute-start | bytes 393224 | tf_op jit(solution)/shard_map/ppermute | solution.py:227
  94.1 0.8 collective-permute-done.33.refs_2_
  94.9 11.9 %stream_dot.3 = (f32[128,4096]{1,0:T(8,128)S(1)}, f32[128,4096]{1,0:T(8,128)S(1)}) custom-call(bf16[32,2048]{1,0:T(8,128)(2,1)S(1)} %get-tuple-element.121.refs_0_, bf16[32,2048]{1,0:T(8,128)(2,1)S(1)} %collective-permute-done.32.refs_1_, bf16[32,2048]{1,0:T(8,128)(2,1)S(1)} %collective-permute-done.33.refs_2_, ...), custom_call_target="tpu_custom_call" | custom-call | flops 4294967296 | bytes 29360128 | tf_op jit(solution)/shard_map/stream_dot/pallas_call | solution.py:29
  106.9 2.4 %held_dot.7 = (bf16[64,4096]{1,0:T(8,128)(2,1)S(1)}, f32[64,4096]{1,0:T(8,128)S(1)}) custom-call(bf16[32,2048]{1,0:T(8,128)(2,1)S(1)} %get-tuple-element.115.refs_0_, bf16[32,2048]{1,0:T(8,128)(2,1)S(1)} %collective-permute-done.28.refs_1_, bf16[32,2048]{1,0:T(8,128)(2,1)S(1)} %collective-permute-done.29.refs_2_, ...), custom_call_target="tpu_custom_call" | custom-call | flops 2147483648 | tf_op jit(solution)/shard_map/held_dot/pallas_call | solution.py:29
  109.4 2.4 %held_dot.6 = (bf16[64,4096]{1,0:T(8,128)(2,1)S(1)}, f32[64,4096]{1,0:T(8,128)S(1)}) custom-call(bf16[32,2048]{1,0:T(8,128)(2,1)S(1)} %get-tuple-element.115.refs_0_, bf16[32,2048]{1,0:T(8,128)(2,1)S(1)} %collective-permute-done.28.refs_1_, bf16[32,2048]{1,0:T(8,128)(2,1)S(1)} %collective-permute-done.29.refs_2_, ...), custom_call_target="tpu_custom_call" | custom-call | flops 2147483648 | tf_op jit(solution)/shard_map/held_dot/pallas_call | solution.py:29
  111.8 0.6 collective-permute-start.35
  112.5 1.1 collective-permute-start.40
  113.5 1.7 %collective-permute-start.41 = (bf16[16,4096]{1,0:T(8,128)(2,1)S(1)}, bf16[16,4096]{1,0:T(8,128)(2,1)S(1)}, u32[]{:S(2)}, u32[]{:S(2)}) collective-permute-start(bf16[16,4096]{1,0:T(8,128)(2,1)S(1)} %get-tuple-element.137), channel_id=1, source_target_pairs={{0,4},{1,5},{2,6},{3,7},{4,0},{5,1},{6,2},{7,3},{8,12},{9,13},{10,... | collective-permute-start | bytes 393224 | tf_op jit(solution)/shard_map/ppermute | solution.py:232
  115.3 0.7 collective-permute-start.42
  116.1 1.1 collective-permute-start.36
  117.2 1.7 %collective-permute-start.37 = (bf16[16,4096]{1,0:T(8,128)(2,1)S(1)}, bf16[16,4096]{1,0:T(8,128)(2,1)S(1)}, u32[]{:S(2)}, u32[]{:S(2)}) collective-permute-start(bf16[16,4096]{1,0:T(8,128)(2,1)S(1)} %get-tuple-element.130), channel_id=1, source_target_pairs={{0,4},{1,5},{2,6},{3,7},{4,0},{5,1},{6,2},{7,3},{8,12},{9,13},{10,... | collective-permute-start | bytes 393224 | tf_op jit(solution)/shard_map/ppermute | solution.py:232
  118.9 2.1 %collective-permute-start.38 = (bf16[16,4096]{1,0:T(8,128)(2,1)S(1)}, bf16[16,4096]{1,0:T(8,128)(2,1)S(1)}, u32[]{:S(2)}, u32[]{:S(2)}) collective-permute-start(bf16[16,4096]{1,0:T(8,128)(2,1)S(1)} %get-tuple-element.131), channel_id=1, source_target_pairs={{0,6},{1,7},{2,4},{3,5},{4,2},{5,3},{6,0},{7,1},{8,14},{9,15},{10,... | collective-permute-start | bytes 393224 | tf_op jit(solution)/shard_map/ppermute | solution.py:232
  121.1 0.6 collective-permute-done.41
  121.7 1.0 collective-permute-done.42
  122.7 1.8 %collective-permute-done.36 = bf16[16,4096]{1,0:T(8,128)(2,1)S(1)} collective-permute-done((bf16[16,4096]{1,0:T(8,128)(2,1)S(1)}, bf16[16,4096]{1,0:T(8,128)(2,1)S(1)}, u32[]{:S(2)}, u32[]{:S(2)}) %collective-permute-start.36) | collective-permute-done | bytes 131104 | tf_op jit(solution)/shard_map/ppermute | solution.py:232
  124.5 1.9 %collective-permute-done.37 = bf16[16,4096]{1,0:T(8,128)(2,1)S(1)} collective-permute-done((bf16[16,4096]{1,0:T(8,128)(2,1)S(1)}, bf16[16,4096]{1,0:T(8,128)(2,1)S(1)}, u32[]{:S(2)}, u32[]{:S(2)}) %collective-permute-start.37) | collective-permute-done | bytes 131104 | tf_op jit(solution)/shard_map/ppermute | solution.py:232
  126.4 0.7 collective-permute-done.38
  127.3 0.7 pad_maximum_fusion
  (59 shorter events, 1.7 us)
Async XLA Ops:
  1.0 1.5 %collective-permute-start = (bf16[16,4096]{1,0:T(8,128)(2,1)S(1)}, bf16[16,4096]{1,0:T(8,128)(2,1)S(1)}, u32[]{:S(2)}, u32[]{:S(2)}) collective-permute-start(bf16[16,4096]{1,0:T(8,128)(2,1)S(1)} %broadcast_select_fusion.6), channel_id=1, source_target_pairs={{0,1},{1,0},{2,3},{3,2},{4,5},{5,4},{6,7},{7,6},{8,9},{9,8},{10,11... | collective-permute-start | bytes 393224 | tf_op jit(solution)/shard_map/ppermute | solution.py:204
  3.5 11.5 %collective-permute-start.2 = (bf16[32,2048]{1,0:T(8,128)(2,1)S(1)}, bf16[32,2048]{1,0:T(8,128)(2,1)S(1)}, u32[]{:S(2)}, u32[]{:S(2)}) collective-permute-start(bf16[32,2048]{1,0:T(8,128)(2,1)S(1)} %pad_maximum_fusion.2.after_ref.refs_0_), channel_id=1, source_target_pairs={{0,8},{8,0},{16,24},{24,16},{1,9},{9,1},{17,25},{25,17},{2,10},{10... | collective-permute-start | bytes 393224 | tf_op jit(solution)/shard_map/ppermute | solution.py:214
  6.5 9.0 %collective-permute-start.1 = (bf16[32,2048]{1,0:T(8,128)(2,1)S(1)}, bf16[32,2048]{1,0:T(8,128)(2,1)S(1)}, u32[]{:S(2)}, u32[]{:S(2)}) collective-permute-start(bf16[32,2048]{1,0:T(8,128)(2,1)S(1)} %pad_maximum_fusion.2.after_ref.refs_0_), channel_id=1, source_target_pairs={{0,16},{8,24},{16,0},{24,8},{1,17},{9,25},{17,1},{25,9},{2,18},{10... | collective-permute-start | bytes 393224 | tf_op jit(solution)/shard_map/ppermute | solution.py:214
  15.6 15.9 %copy-start = (f32[16,8192]{1,0:T(8,128)S(1)}, f32[16,8192]{1,0:T(8,128)}, u32[]{:S(2)}) copy-start(f32[16,8192]{1,0:T(8,128)} %param.5) | copy-start | bytes 1572868
  15.6 15.9 %copy-start.1 = (f32[16,8192]{1,0:T(8,128)S(1)}, f32[16,8192]{1,0:T(8,128)}, u32[]{:S(2)}) copy-start(f32[16,8192]{1,0:T(8,128)} %param.6) | copy-start | bytes 1572868
  15.6 10.2 %collective-permute-start.10 = (bf16[32,2048]{1,0:T(8,128)(2,1)S(1)}, bf16[32,2048]{1,0:T(8,128)(2,1)S(1)}, u32[]{:S(2)}, u32[]{:S(2)}) collective-permute-start(bf16[32,2048]{1,0:T(8,128)(2,1)S(1)} %collective-permute-done.1.after_ref.refs_2_), channel_id=1, source_target_pairs={{0,8},{8,0},{16,24},{24,16},{1,9},{9,1},{17,25},{25,17},{2,10},{10... | collective-permute-start | bytes 393224 | tf_op jit(solution)/shard_map/ppermute | solution.py:220
  16.0 13.4 %collective-permute-start.3 = (bf16[32,2048]{1,0:T(8,128)(2,1)S(1)}, bf16[32,2048]{1,0:T(8,128)(2,1)S(1)}, u32[]{:S(2)}, u32[]{:S(2)}) collective-permute-start(bf16[32,2048]{1,0:T(8,128)(2,1)S(1)} %pad_maximum_fusion.1.refs_0_), channel_id=1, source_target_pairs={{0,16},{8,24},{16,0},{24,8},{1,17},{9,25},{17,1},{25,9},{2,18},{10... | collective-permute-start | bytes 393224 | tf_op jit(solution)/shard_map/ppermute | solution.py:214
  18.6 12.9 %collective-permute-start.5 = (bf16[32,2048]{1,0:T(8,128)(2,1)S(1)}, bf16[32,2048]{1,0:T(8,128)(2,1)S(1)}, u32[]{:S(2)}, u32[]{:S(2)}) collective-permute-start(bf16[32,2048]{1,0:T(8,128)(2,1)S(1)} %pad_maximum_fusion.1.refs_0_), channel_id=1, source_target_pairs={{0,8},{8,0},{16,24},{24,16},{1,9},{9,1},{17,25},{25,17},{2,10},{10... | collective-permute-start | bytes 393224 | tf_op jit(solution)/shard_map/ppermute | solution.py:214
  25.9 8.6 %collective-permute-start.11 = (bf16[32,2048]{1,0:T(8,128)(2,1)S(1)}, bf16[32,2048]{1,0:T(8,128)(2,1)S(1)}, u32[]{:S(2)}, u32[]{:S(2)}) collective-permute-start(bf16[32,2048]{1,0:T(8,128)(2,1)S(1)} %get-tuple-element.95), channel_id=1, source_target_pairs={{0,2},{1,3},{2,0},{3,1},{4,6},{5,7},{6,4},{7,5},{8,10},{9,11},{10,... | collective-permute-start | bytes 393224 | tf_op jit(solution)/shard_map/ppermute | solution.py:227
  27.5 8.6 %collective-permute-start.12 = (bf16[32,2048]{1,0:T(8,128)(2,1)S(1)}, bf16[32,2048]{1,0:T(8,128)(2,1)S(1)}, u32[]{:S(2)}, u32[]{:S(2)}) collective-permute-start(bf16[32,2048]{1,0:T(8,128)(2,1)S(1)} %get-tuple-element.96), channel_id=1, source_target_pairs={{0,4},{1,5},{2,6},{3,7},{4,0},{5,1},{6,2},{7,3},{8,12},{9,13},{10,... | collective-permute-start | bytes 393224 | tf_op jit(solution)/shard_map/ppermute | solution.py:227
  29.0 8.6 %collective-permute-start.13 = (bf16[32,2048]{1,0:T(8,128)(2,1)S(1)}, bf16[32,2048]{1,0:T(8,128)(2,1)S(1)}, u32[]{:S(2)}, u32[]{:S(2)}) collective-permute-start(bf16[32,2048]{1,0:T(8,128)(2,1)S(1)} %get-tuple-element.97), channel_id=1, source_target_pairs={{0,6},{1,7},{2,4},{3,5},{4,2},{5,3},{6,0},{7,1},{8,14},{9,15},{10,... | collective-permute-start | bytes 393224 | tf_op jit(solution)/shard_map/ppermute | solution.py:227
  29.5 5.0 %collective-permute-start.6 = (bf16[32,2048]{1,0:T(8,128)(2,1)S(1)}, bf16[32,2048]{1,0:T(8,128)(2,1)S(1)}, u32[]{:S(2)}, u32[]{:S(2)}) collective-permute-start(bf16[32,2048]{1,0:T(8,128)(2,1)S(1)} %collective-permute-done.3.refs_2_), channel_id=1, source_target_pairs={{0,8},{8,0},{16,24},{24,16},{1,9},{9,1},{17,25},{25,17},{2,10},{10... | collective-permute-start | bytes 393224 | tf_op jit(solution)/shard_map/ppermute | solution.py:220
  31.5 18.5 %collective-permute-start.18 = (f32[16,4096]{1,0:T(8,128)S(1)}, f32[16,4096]{1,0:T(8,128)S(1)}, u32[]{:S(2)}, u32[]{:S(2)}) collective-permute-start(f32[16,4096]{1,0:T(8,128)S(1)} %slice_select_fusion), channel_id=1, source_target_pairs={{0,1},{1,0},{2,3},{3,2},{4,5},{5,4},{6,7},{7,6},{8,9},{9,8},{10,11... | collective-permute-start | bytes 786440 | tf_op jit(solution)/shard_map/ppermute | solution.py:204
  34.4 21.3 %collective-permute-start.4 = (f32[16,4096]{1,0:T(8,128)S(1)}, f32[16,4096]{1,0:T(8,128)S(1)}, u32[]{:S(2)}, u32[]{:S(2)}) collective-permute-start(f32[16,4096]{1,0:T(8,128)S(1)} %slice_select_fusion.2), channel_id=1, source_target_pairs={{0,1},{1,0},{2,3},{3,2},{4,5},{5,4},{6,7},{7,6},{8,9},{9,8},{10,11... | collective-permute-start | bytes 786440 | tf_op jit(solution)/shard_map/ppermute | solution.py:204
  34.5 15.6 %collective-permute-start.7 = (bf16[32,2048]{1,0:T(8,128)(2,1)S(1)}, bf16[32,2048]{1,0:T(8,128)(2,1)S(1)}, u32[]{:S(2)}, u32[]{:S(2)}) collective-permute-start(bf16[32,2048]{1,0:T(8,128)(2,1)S(1)} %get-tuple-element.82), channel_id=1, source_target_pairs={{0,2},{1,3},{2,0},{3,1},{4,6},{5,7},{6,4},{7,5},{8,10},{9,11},{10,... | collective-permute-start | bytes 393224 | tf_op jit(solution)/shard_map/ppermute | solution.py:227
  36.1 14.0 %collective-permute-start.8 = (bf16[32,2048]{1,0:T(8,128)(2,1)S(1)}, bf16[32,2048]{1,0:T(8,128)(2,1)S(1)}, u32[]{:S(2)}, u32[]{:S(2)}) collective-permute-start(bf16[32,2048]{1,0:T(8,128)(2,1)S(1)} %get-tuple-element.83), channel_id=1, source_target_pairs={{0,4},{1,5},{2,6},{3,7},{4,0},{5,1},{6,2},{7,3},{8,12},{9,13},{10,... | collective-permute-start | bytes 393224 | tf_op jit(solution)/shard_map/ppermute | solution.py:227
  37.6 12.5 %collective-permute-start.9 = (bf16[32,2048]{1,0:T(8,128)(2,1)S(1)}, bf16[32,2048]{1,0:T(8,128)(2,1)S(1)}, u32[]{:S(2)}, u32[]{:S(2)}) collective-permute-start(bf16[32,2048]{1,0:T(8,128)(2,1)S(1)} %get-tuple-element.84), channel_id=1, source_target_pairs={{0,6},{1,7},{2,4},{3,5},{4,2},{5,3},{6,0},{7,1},{8,14},{9,15},{10,... | collective-permute-start | bytes 393224 | tf_op jit(solution)/shard_map/ppermute | solution.py:227
  52.6 3.2 %collective-permute-start.19 = (bf16[128,2048]{1,0:T(8,128)(2,1)S(1)}, bf16[128,2048]{1,0:T(8,128)(2,1)S(1)}, u32[]{:S(2)}, u32[]{:S(2)}) collective-permute-start(bf16[128,2048]{1,0:T(8,128)(2,1)S(1)} %get-tuple-element.109), channel_id=1, source_target_pairs={{0,1},{1,0},{2,3},{3,2},{4,5},{5,4},{6,7},{7,6},{8,9},{9,8},{10,11... | collective-permute-start | bytes 1572872 | tf_op jit(solution)/shard_map/ppermute | solution.py:303
  55.2 4.4 %collective-permute-start.14 = (bf16[128,2048]{1,0:T(8,128)(2,1)S(1)}, bf16[128,2048]{1,0:T(8,128)(2,1)S(1)}, u32[]{:S(2)}, u32[]{:S(2)}) collective-permute-start(bf16[128,2048]{1,0:T(8,128)(2,1)S(1)} %get-tuple-element.101), channel_id=1, source_target_pairs={{0,1},{1,0},{2,3},{3,2},{4,5},{5,4},{6,7},{7,6},{8,9},{9,8},{10,11... | collective-permute-start | bytes 1572872 | tf_op jit(solution)/shard_map/ppermute | solution.py:303
  56.0 6.7 %collective-permute-start.20 = (bf16[32,2048]{1,0:T(8,128)(2,1)S(1)}, bf16[32,2048]{1,0:T(8,128)(2,1)S(1)}, u32[]{:S(2)}, u32[]{:S(2)}) collective-permute-start(bf16[32,2048]{1,0:T(8,128)(2,1)S(1)} %get-tuple-element.111), channel_id=1, source_target_pairs={{0,2},{1,3},{2,0},{3,1},{4,6},{5,7},{6,4},{7,5},{8,10},{9,11},{10,... | collective-permute-start | bytes 393224 | tf_op jit(solution)/shard_map/ppermute | solution.py:232
  57.5 8.3 %collective-permute-start.21 = (bf16[32,2048]{1,0:T(8,128)(2,1)S(1)}, bf16[32,2048]{1,0:T(8,128)(2,1)S(1)}, u32[]{:S(2)}, u32[]{:S(2)}) collective-permute-start(bf16[32,2048]{1,0:T(8,128)(2,1)S(1)} %get-tuple-element.112), channel_id=1, source_target_pairs={{0,4},{1,5},{2,6},{3,7},{4,0},{5,1},{6,2},{7,3},{8,12},{9,13},{10,... | collective-permute-start | bytes 393224 | tf_op jit(solution)/shard_map/ppermute | solution.py:232
  59.0 7.4 %collective-permute-start.22 = (bf16[32,2048]{1,0:T(8,128)(2,1)S(1)}, bf16[32,2048]{1,0:T(8,128)(2,1)S(1)}, u32[]{:S(2)}, u32[]{:S(2)}) collective-permute-start(bf16[32,2048]{1,0:T(8,128)(2,1)S(1)} %get-tuple-element.113), channel_id=1, source_target_pairs={{0,6},{1,7},{2,4},{3,5},{4,2},{5,3},{6,0},{7,1},{8,14},{9,15},{10,... | collective-permute-start | bytes 393224 | tf_op jit(solution)/shard_map/ppermute | solution.py:232
  59.7 9.2 %collective-permute-start.15 = (bf16[32,2048]{1,0:T(8,128)(2,1)S(1)}, bf16[32,2048]{1,0:T(8,128)(2,1)S(1)}, u32[]{:S(2)}, u32[]{:S(2)}) collective-permute-start(bf16[32,2048]{1,0:T(8,128)(2,1)S(1)} %get-tuple-element.103), channel_id=1, source_target_pairs={{0,2},{1,3},{2,0},{3,1},{4,6},{5,7},{6,4},{7,5},{8,10},{9,11},{10,... | collective-permute-start | bytes 393224 | tf_op jit(solution)/shard_map/ppermute | solution.py:232
  61.2 9.9 %collective-permute-start.16 = (bf16[32,2048]{1,0:T(8,128)(2,1)S(1)}, bf16[32,2048]{1,0:T(8,128)(2,1)S(1)}, u32[]{:S(2)}, u32[]{:S(2)}) collective-permute-start(bf16[32,2048]{1,0:T(8,128)(2,1)S(1)} %get-tuple-element.104), channel_id=1, source_target_pairs={{0,4},{1,5},{2,6},{3,7},{4,0},{5,1},{6,2},{7,3},{8,12},{9,13},{10,... | collective-permute-start | bytes 393224 | tf_op jit(solution)/shard_map/ppermute | solution.py:232
  62.7 8.4 %collective-permute-start.17 = (bf16[32,2048]{1,0:T(8,128)(2,1)S(1)}, bf16[32,2048]{1,0:T(8,128)(2,1)S(1)}, u32[]{:S(2)}, u32[]{:S(2)}) collective-permute-start(bf16[32,2048]{1,0:T(8,128)(2,1)S(1)} %get-tuple-element.105), channel_id=1, source_target_pairs={{0,6},{1,7},{2,4},{3,5},{4,2},{5,3},{6,0},{7,1},{8,14},{9,15},{10,... | collective-permute-start | bytes 393224 | tf_op jit(solution)/shard_map/ppermute | solution.py:232
  66.5 6.2 %collective-permute-start.24 = (bf16[32,2048]{1,0:T(8,128)(2,1)S(1)}, bf16[32,2048]{1,0:T(8,128)(2,1)S(1)}, u32[]{:S(2)}, u32[]{:S(2)}) collective-permute-start(bf16[32,2048]{1,0:T(8,128)(2,1)S(1)} %fusion.3.refs_0_), channel_id=1, source_target_pairs={{0,8},{8,0},{16,24},{24,16},{1,9},{9,1},{17,25},{25,17},{2,10},{10... | collective-permute-start | bytes 393224 | tf_op jit(solution)/shard_map/ppermute | solution.py:214
  68.5 9.2 %collective-permute-start.23 = (bf16[32,2048]{1,0:T(8,128)(2,1)S(1)}, bf16[32,2048]{1,0:T(8,128)(2,1)S(1)}, u32[]{:S(2)}, u32[]{:S(2)}) collective-permute-start(bf16[32,2048]{1,0:T(8,128)(2,1)S(1)} %fusion.3.refs_0_), channel_id=1, source_target_pairs={{0,16},{8,24},{16,0},{24,8},{1,17},{9,25},{17,1},{25,9},{2,18},{10... | collective-permute-start | bytes 393224 | tf_op jit(solution)/shard_map/ppermute | solution.py:214
  77.7 6.1 %collective-permute-start.26 = (bf16[32,2048]{1,0:T(8,128)(2,1)S(1)}, bf16[32,2048]{1,0:T(8,128)(2,1)S(1)}, u32[]{:S(2)}, u32[]{:S(2)}) collective-permute-start(bf16[32,2048]{1,0:T(8,128)(2,1)S(1)} %fusion.1.refs_0_), channel_id=1, source_target_pairs={{0,16},{8,24},{16,0},{24,8},{1,17},{9,25},{17,1},{25,9},{2,18},{10... | collective-permute-start | bytes 393224 | tf_op jit(solution)/shard_map/ppermute | solution.py:214
  77.7 7.5 %collective-permute-start.31 = (bf16[32,2048]{1,0:T(8,128)(2,1)S(1)}, bf16[32,2048]{1,0:T(8,128)(2,1)S(1)}, u32[]{:S(2)}, u32[]{:S(2)}) collective-permute-start(bf16[32,2048]{1,0:T(8,128)(2,1)S(1)} %collective-permute-done.23.refs_2_), channel_id=1, source_target_pairs={{0,8},{8,0},{16,24},{24,16},{1,9},{9,1},{17,25},{25,17},{2,10},{10... | collective-permute-start | bytes 393224 | tf_op jit(solution)/shard_map/ppermute | solution.py:220
  79.2 10.3 %collective-permute-start.25 = (bf16[32,2048]{1,0:T(8,128)(2,1)S(1)}, bf16[32,2048]{1,0:T(8,128)(2,1)S(1)}, u32[]{:S(2)}, u32[]{:S(2)}) collective-permute-start(bf16[32,2048]{1,0:T(8,128)(2,1)S(1)} %fusion.1.refs_0_), channel_id=1, source_target_pairs={{0,8},{8,0},{16,24},{24,16},{1,9},{9,1},{17,25},{25,17},{2,10},{10... | collective-permute-start | bytes 393224 | tf_op jit(solution)/shard_map/ppermute | solution.py:214
  83.8 5.7 %collective-permute-start.27 = (bf16[32,2048]{1,0:T(8,128)(2,1)S(1)}, bf16[32,2048]{1,0:T(8,128)(2,1)S(1)}, u32[]{:S(2)}, u32[]{:S(2)}) collective-permute-start(bf16[32,2048]{1,0:T(8,128)(2,1)S(1)} %collective-permute-done.26.refs_2_), channel_id=1, source_target_pairs={{0,8},{8,0},{16,24},{24,16},{1,9},{9,1},{17,25},{25,17},{2,10},{10... | collective-permute-start | bytes 393224 | tf_op jit(solution)/shard_map/ppermute | solution.py:220
  85.3 7.5 %collective-permute-start.32 = (bf16[32,2048]{1,0:T(8,128)(2,1)S(1)}, bf16[32,2048]{1,0:T(8,128)(2,1)S(1)}, u32[]{:S(2)}, u32[]{:S(2)}) collective-permute-start(bf16[32,2048]{1,0:T(8,128)(2,1)S(1)} %get-tuple-element.122), channel_id=1, source_target_pairs={{0,2},{1,3},{2,0},{3,1},{4,6},{5,7},{6,4},{7,5},{8,10},{9,11},{10,... | collective-permute-start | bytes 393224 | tf_op jit(solution)/shard_map/ppermute | solution.py:227
  86.7 8.3 %collective-permute-start.33 = (bf16[32,2048]{1,0:T(8,128)(2,1)S(1)}, bf16[32,2048]{1,0:T(8,128)(2,1)S(1)}, u32[]{:S(2)}, u32[]{:S(2)}) collective-permute-start(bf16[32,2048]{1,0:T(8,128)(2,1)S(1)} %get-tuple-element.123), channel_id=1, source_target_pairs={{0,4},{1,5},{2,6},{3,7},{4,0},{5,1},{6,2},{7,3},{8,12},{9,13},{10,... | collective-permute-start | bytes 393224 | tf_op jit(solution)/shard_map/ppermute | solution.py:227
  88.1 6.8 %collective-permute-start.34 = (bf16[32,2048]{1,0:T(8,128)(2,1)S(1)}, bf16[32,2048]{1,0:T(8,128)(2,1)S(1)}, u32[]{:S(2)}, u32[]{:S(2)}) collective-permute-start(bf16[32,2048]{1,0:T(8,128)(2,1)S(1)} %get-tuple-element.124), channel_id=1, source_target_pairs={{0,6},{1,7},{2,4},{3,5},{4,2},{5,3},{6,0},{7,1},{8,14},{9,15},{10,... | collective-permute-start | bytes 393224 | tf_op jit(solution)/shard_map/ppermute | solution.py:227
  89.8 17.0 %collective-permute-start.28 = (bf16[32,2048]{1,0:T(8,128)(2,1)S(1)}, bf16[32,2048]{1,0:T(8,128)(2,1)S(1)}, u32[]{:S(2)}, u32[]{:S(2)}) collective-permute-start(bf16[32,2048]{1,0:T(8,128)(2,1)S(1)} %get-tuple-element.116), channel_id=1, source_target_pairs={{0,2},{1,3},{2,0},{3,1},{4,6},{5,7},{6,4},{7,5},{8,10},{9,11},{10,... | collective-permute-start | bytes 393224 | tf_op jit(solution)/shard_map/ppermute | solution.py:227
  90.5 16.4 %collective-permute-start.29 = (bf16[32,2048]{1,0:T(8,128)(2,1)S(1)}, bf16[32,2048]{1,0:T(8,128)(2,1)S(1)}, u32[]{:S(2)}, u32[]{:S(2)}) collective-permute-start(bf16[32,2048]{1,0:T(8,128)(2,1)S(1)} %get-tuple-element.117), channel_id=1, source_target_pairs={{0,4},{1,5},{2,6},{3,7},{4,0},{5,1},{6,2},{7,3},{8,12},{9,13},{10,... | collective-permute-start | bytes 393224 | tf_op jit(solution)/shard_map/ppermute | solution.py:227
  92.8 14.1 %collective-permute-start.30 = (bf16[32,2048]{1,0:T(8,128)(2,1)S(1)}, bf16[32,2048]{1,0:T(8,128)(2,1)S(1)}, u32[]{:S(2)}, u32[]{:S(2)}) collective-permute-start(bf16[32,2048]{1,0:T(8,128)(2,1)S(1)} %get-tuple-element.118), channel_id=1, source_target_pairs={{0,6},{1,7},{2,4},{3,5},{4,2},{5,3},{6,0},{7,1},{8,14},{9,15},{10,... | collective-permute-start | bytes 393224 | tf_op jit(solution)/shard_map/ppermute | solution.py:227
  109.3 3.1 %collective-permute-start.39 = (bf16[64,4096]{1,0:T(8,128)(2,1)S(1)}, bf16[64,4096]{1,0:T(8,128)(2,1)S(1)}, u32[]{:S(2)}, u32[]{:S(2)}) collective-permute-start(bf16[64,4096]{1,0:T(8,128)(2,1)S(1)} %get-tuple-element.134), channel_id=1, source_target_pairs={{0,1},{1,0},{2,3},{3,2},{4,5},{5,4},{6,7},{7,6},{8,9},{9,8},{10,11... | collective-permute-start | bytes 1572872 | tf_op jit(solution)/shard_map/ppermute | solution.py:303
  111.8 4.2 %collective-permute-start.35 = (bf16[64,4096]{1,0:T(8,128)(2,1)S(1)}, bf16[64,4096]{1,0:T(8,128)(2,1)S(1)}, u32[]{:S(2)}, u32[]{:S(2)}) collective-permute-start(bf16[64,4096]{1,0:T(8,128)(2,1)S(1)} %get-tuple-element.127), channel_id=1, source_target_pairs={{0,1},{1,0},{2,3},{3,2},{4,5},{5,4},{6,7},{7,6},{8,9},{9,8},{10,11... | collective-permute-start | bytes 1572872 | tf_op jit(solution)/shard_map/ppermute | solution.py:303
  112.5 6.5 %collective-permute-start.40 = (bf16[16,4096]{1,0:T(8,128)(2,1)S(1)}, bf16[16,4096]{1,0:T(8,128)(2,1)S(1)}, u32[]{:S(2)}, u32[]{:S(2)}) collective-permute-start(bf16[16,4096]{1,0:T(8,128)(2,1)S(1)} %get-tuple-element.136), channel_id=1, source_target_pairs={{0,2},{1,3},{2,0},{3,1},{4,6},{5,7},{6,4},{7,5},{8,10},{9,11},{10,... | collective-permute-start | bytes 393224 | tf_op jit(solution)/shard_map/ppermute | solution.py:232
  113.5 8.1 %collective-permute-start.41 = (bf16[16,4096]{1,0:T(8,128)(2,1)S(1)}, bf16[16,4096]{1,0:T(8,128)(2,1)S(1)}, u32[]{:S(2)}, u32[]{:S(2)}) collective-permute-start(bf16[16,4096]{1,0:T(8,128)(2,1)S(1)} %get-tuple-element.137), channel_id=1, source_target_pairs={{0,4},{1,5},{2,6},{3,7},{4,0},{5,1},{6,2},{7,3},{8,12},{9,13},{10,... | collective-permute-start | bytes 393224 | tf_op jit(solution)/shard_map/ppermute | solution.py:232
  115.3 7.4 %collective-permute-start.42 = (bf16[16,4096]{1,0:T(8,128)(2,1)S(1)}, bf16[16,4096]{1,0:T(8,128)(2,1)S(1)}, u32[]{:S(2)}, u32[]{:S(2)}) collective-permute-start(bf16[16,4096]{1,0:T(8,128)(2,1)S(1)} %get-tuple-element.138), channel_id=1, source_target_pairs={{0,6},{1,7},{2,4},{3,5},{4,2},{5,3},{6,0},{7,1},{8,14},{9,15},{10,... | collective-permute-start | bytes 393224 | tf_op jit(solution)/shard_map/ppermute | solution.py:232
  116.1 8.4 %collective-permute-start.36 = (bf16[16,4096]{1,0:T(8,128)(2,1)S(1)}, bf16[16,4096]{1,0:T(8,128)(2,1)S(1)}, u32[]{:S(2)}, u32[]{:S(2)}) collective-permute-start(bf16[16,4096]{1,0:T(8,128)(2,1)S(1)} %get-tuple-element.129), channel_id=1, source_target_pairs={{0,2},{1,3},{2,0},{3,1},{4,6},{5,7},{6,4},{7,5},{8,10},{9,11},{10,... | collective-permute-start | bytes 393224 | tf_op jit(solution)/shard_map/ppermute | solution.py:232
  117.2 9.2 %collective-permute-start.37 = (bf16[16,4096]{1,0:T(8,128)(2,1)S(1)}, bf16[16,4096]{1,0:T(8,128)(2,1)S(1)}, u32[]{:S(2)}, u32[]{:S(2)}) collective-permute-start(bf16[16,4096]{1,0:T(8,128)(2,1)S(1)} %get-tuple-element.130), channel_id=1, source_target_pairs={{0,4},{1,5},{2,6},{3,7},{4,0},{5,1},{6,2},{7,3},{8,12},{9,13},{10,... | collective-permute-start | bytes 393224 | tf_op jit(solution)/shard_map/ppermute | solution.py:232
  118.9 8.2 %collective-permute-start.38 = (bf16[16,4096]{1,0:T(8,128)(2,1)S(1)}, bf16[16,4096]{1,0:T(8,128)(2,1)S(1)}, u32[]{:S(2)}, u32[]{:S(2)}) collective-permute-start(bf16[16,4096]{1,0:T(8,128)(2,1)S(1)} %get-tuple-element.131), channel_id=1, source_target_pairs={{0,6},{1,7},{2,4},{3,5},{4,2},{5,3},{6,0},{7,1},{8,14},{9,15},{10,... | collective-permute-start | bytes 393224 | tf_op jit(solution)/shard_map/ppermute | solution.py:232
